TPU v7x, 128 devices: a whole 4x4x4 slice. The times are simulated.
128 devices in a mesh: seq: 16 (over x_hi, y, core), tp: 8 (over z, x_lo).
Axes of the slice: x: 4 (x_hi: 2, x_lo: 2; x = x_hi * 2 + x_lo), y: 4, z: 4, core: 2. Of those that a mesh axis runs over, the one named last changes fastest.
Arguments:
- fine_stream: bfloat16 [16384, 2048], P(('seq', 'tp')), may hold values from -20 to 20
- queries: bfloat16 [16384, 1024], P(('seq', 'tp')), may hold values from -80 to 80
- keys: bfloat16 [16384, 1024], P(('seq', 'tp')), may hold values from -8 to 8
- values: bfloat16 [16384, 1024], P(('seq', 'tp')), may hold values from -6 to 6
- out_weight: bfloat16 [1024, 2048], replicated, may hold values from -0.1875 to 0.1875
- norm_gain: float32 [2048], replicated, may hold values from 0.25 to 1.75
- gate_weight: bfloat16 [2048, 5632], P(None, 'tp'), may hold values from -0.125 to 0.125
- up_weight: bfloat16 [2048, 5632], P(None, 'tp'), may hold values from -0.125 to 0.125
- down_weight: bfloat16 [5632, 2048], P('tp'), may hold values from -0.078125 to 0.078125
- cotangent: bfloat16 [16384, 2048], P(('seq', 'tp')), may hold values from -12 to 12
Outputs:
- section_out: bfloat16 [16384, 2048], P(('seq', 'tp'))
- stream_grad: bfloat16 [16384, 2048], P(('seq', 'tp'))
- gate_grad: float32 [2048, 5632], P('seq', 'tp')
- up_grad: float32 [2048, 5632], P('seq', 'tp')
- down_grad: float32 [5632, 2048], P('tp', 'seq')
- gain_grad: float32 [2048], replicated
All inputs are finite; a program needn't handle non-finite values.
Results may differ from a plain program's by a relative error of at most 0.02.
Values may be sent and summed in bfloat16 or wider, within the bound.
A program may use at most 128 MiB of HBM per device.

v0:
```python
import jax
import jax.numpy as jnp
from jax import lax
from jax.sharding import PartitionSpec as P

D = 2048
HEAD = 128
SHORTEN = 8


contract_last = (((1,), (1,)), ((), ()))
contract_first = (((0,), (0,)), ((), ()))
very_low = -1e30


def shifted(value, axis, steps):
    count = lax.axis_size(axis)
    leading, last = (max(0, -steps), min(count, count - steps))
    return lax.ppermute(value, axis, [(source, source + steps) for source in range(leading, last)])


def on_device(
    fine_stream,
    queries,
    keys,
    values,
    out_weight,
    norm_gain,
    gate_weight,
    up_weight,
    down_weight,
    cotangent,
):
    tok = fine_stream.shape[0]
    q_heads, k_heads, v_heads = (
        lax.all_to_all(queries, "tp", split_axis=1, concat_axis=0, tiled=True),
        lax.all_to_all(keys, "tp", split_axis=1, concat_axis=0, tiled=True),
        lax.all_to_all(values, "tp", split_axis=1, concat_axis=0, tiled=True),
    )
    group_rows = q_heads.shape[0]
    heads_here = q_heads.shape[1] // HEAD
    group_start = lax.axis_index("seq") * group_rows
    query_pos = group_start + jnp.arange(group_rows, dtype=jnp.int32)
    last_query = group_start + group_rows - 1
    q_split = q_heads.reshape(group_rows, heads_here, HEAD)

    def attend_block(carry, key_block, value_block, key_start):
        maxima, totals, summed = carry
        scores = jnp.einsum(
            "qhd,khd->hqk",
            q_split,
            key_block.reshape(-1, heads_here, HEAD),
            preferred_element_type=jnp.float32,
        ) * HEAD ** (-0.5)
        key_pos = key_start + jnp.arange(key_block.shape[0], dtype=jnp.int32)
        visible = (query_pos[:, None] >= key_pos[None, :])[None]
        masked = jnp.where(visible, scores, very_low)
        fresh = jnp.maximum(maxima, jnp.max(masked, axis=-1))
        weights = jnp.where(visible, jnp.exp(masked - fresh[..., None]), 0.0)
        factor = jnp.exp(maxima - fresh)
        totals = totals * factor + jnp.sum(weights, axis=-1)
        mixed = jnp.einsum(
            "hqk,khd->qhd",
            weights.astype(jnp.bfloat16),
            value_block.reshape(-1, heads_here, HEAD),
            preferred_element_type=jnp.float32,
        )
        summed = summed * factor.T[..., None] + mixed
        return (fresh, totals, summed)

    initial = (
        jnp.full((heads_here, group_rows), very_low, jnp.float32),
        jnp.zeros((heads_here, group_rows), jnp.float32),
        jnp.zeros((group_rows, heads_here, HEAD), jnp.float32),
    )
    key_piece = lax.all_gather(k_heads, "seq", axis=0, tiled=True)
    value_piece = lax.all_gather(v_heads, "seq", axis=0, tiled=True)
    width = min(group_rows, key_piece.shape[0])
    blocks = key_piece.shape[0] // width

    def one_block(index, inner):
        offset = index * width
        key_block = lax.dynamic_slice_in_dim(key_piece, offset, width, 0)
        value_block = lax.dynamic_slice_in_dim(value_piece, offset, width, 0)
        return lax.cond(
            offset <= last_query,
            lambda c: attend_block(c, key_block, value_block, offset),
            lambda c: c,
            inner,
        )

    maxima, totals, summed = lax.fori_loop(0, blocks, one_block, initial)
    attn_heads = (
        (summed / totals.T[..., None]).reshape(group_rows, heads_here * HEAD).astype(jnp.bfloat16)
    )
    attention = lax.all_to_all(attn_heads, "tp", split_axis=0, concat_axis=1, tiled=True)
    projected = jnp.dot(attention, out_weight, preferred_element_type=jnp.float32)
    stream = (fine_stream.astype(jnp.float32) + projected).astype(jnp.bfloat16)
    crows = tok // SHORTEN
    border = shifted(stream[tok - SHORTEN :], ("seq", "tp"), 1)
    extended = jnp.concatenate([border[1:], stream], 0)[:tok]
    coarse = extended.astype(jnp.float32).reshape(crows, SHORTEN, D).sum(1) / SHORTEN
    rstd = lax.rsqrt(jnp.mean(coarse * coarse, axis=-1, keepdims=True) + 1e-05)
    base = coarse * rstd
    normed = (base * norm_gain).astype(jnp.bfloat16)
    normed_group = lax.all_gather(normed, "tp", axis=0, tiled=True)
    gate = jnp.dot(normed_group, gate_weight, preferred_element_type=jnp.float32)
    up = jnp.dot(normed_group, up_weight, preferred_element_type=jnp.float32)
    sig = jax.nn.sigmoid(gate)
    hidden = (gate * sig * up).astype(jnp.bfloat16)
    coarse_out = coarse + lax.psum_scatter(
        jnp.dot(hidden, down_weight, preferred_element_type=jnp.float32).astype(jnp.bfloat16),
        "tp",
        scatter_dimension=0,
        tiled=True,
    ).astype(jnp.float32)
    section_out = (
        (stream.astype(jnp.float32).reshape(crows, SHORTEN, D) + coarse_out[:, None, :])
        .reshape(tok, D)
        .astype(jnp.bfloat16)
    )
    grad = cotangent.astype(jnp.float32)
    coarse_grad = grad.reshape(crows, SHORTEN, D).sum(1)
    coarse_grad_b = coarse_grad.astype(jnp.bfloat16)
    grad_group = lax.all_gather(coarse_grad_b, "tp", axis=0, tiled=True)
    hidden_grad = lax.dot_general(
        grad_group, down_weight, contract_last, preferred_element_type=jnp.float32
    )
    gate_delta = (hidden_grad * up * sig * (1.0 + gate * (1.0 - sig))).astype(jnp.bfloat16)
    up_delta = (hidden_grad * gate * sig).astype(jnp.bfloat16)
    normed_grad = lax.psum_scatter(
        (
            lax.dot_general(
                gate_delta, gate_weight, contract_last, preferred_element_type=jnp.float32
            )
            + lax.dot_general(
                up_delta, up_weight, contract_last, preferred_element_type=jnp.float32
            )
        ).astype(jnp.bfloat16),
        "tp",
        scatter_dimension=0,
        tiled=True,
    ).astype(jnp.float32)
    gain_grad = lax.psum(jnp.sum(normed_grad * base, axis=0), ("seq", "tp"))
    scaled = normed_grad * norm_gain
    coarse_total = coarse_grad + rstd * (
        scaled - base * jnp.mean(scaled * base, axis=-1, keepdims=True)
    )
    following = shifted(coarse_total[:1], ("seq", "tp"), -1)
    ahead = jnp.concatenate([coarse_total[1:], following], 0)
    spread = jnp.broadcast_to(ahead[:, None, :], (crows, SHORTEN, D)).reshape(tok, D)
    contrib = jnp.concatenate([coarse_total[:1], spread[: tok - 1]], 0)
    stream_grad = (grad + contrib / SHORTEN).astype(jnp.bfloat16)
    gate_local = lax.dot_general(
        normed_group, gate_delta, contract_first, preferred_element_type=jnp.float32
    )
    up_local = lax.dot_general(
        normed_group, up_delta, contract_first, preferred_element_type=jnp.float32
    )
    gate_grad, up_grad = (
        lax.psum_scatter(
            gate_local.astype(jnp.bfloat16), "seq", scatter_dimension=0, tiled=True
        ).astype(jnp.float32),
        lax.psum_scatter(
            up_local.astype(jnp.bfloat16), "seq", scatter_dimension=0, tiled=True
        ).astype(jnp.float32),
    )
    down_local = lax.dot_general(
        hidden, grad_group, contract_first, preferred_element_type=jnp.float32
    )
    down_grad = lax.psum_scatter(
        down_local.astype(jnp.bfloat16), "seq", scatter_dimension=1, tiled=True
    ).astype(jnp.float32)
    return (section_out, stream_grad, gate_grad, up_grad, down_grad, gain_grad)


def solution(mesh):
    return jax.shard_map(
        on_device,
        mesh=mesh,
        in_specs=(
            P(("seq", "tp"), None),
            P(("seq", "tp"), None),
            P(("seq", "tp"), None),
            P(("seq", "tp"), None),
            P(),
            P(),
            P(None, "tp"),
            P(None, "tp"),
            P("tp", None),
            P(("seq", "tp"), None),
        ),
        out_specs=(
            P(("seq", "tp"), None),
            P(("seq", "tp"), None),
            P("seq", "tp"),
            P("seq", "tp"),
            P("tp", "seq"),
            P(),
        ),
        check_vma=False,
    )
```

profile of v0, /device:TPU:0, one launch (start us, length us, event | category | flops | bytes accessed | tf_op | source)
XLA Modules:
  0.0 624.7 jit_solution(17128821391324157516)
XLA Ops:
  8.4 13.5 %all_to_all.70 = bf16[128,8,128]{2,0,1:T(8,128)(2,1)} all-to-all(bf16[128,8,128]{2,0,1:T(8,128)(2,1)S(1)} %copy_bitcast_fusion.1), channel_id=1, replica_groups=mesh['seq'=16,'tp'=8] {'tp'}, dimensions={1} | all-to-all | bytes 524288 | tf_op jit(solution)/shard_map/all_to_all | solution.py:37
  23.0 10.4 %all_to_all.71 = bf16[128,8,128]{2,0,1:T(8,128)(2,1)} all-to-all(bf16[128,8,128]{2,0,1:T(8,128)(2,1)S(1)} %copy_bitcast_fusion), channel_id=1, replica_groups=mesh['seq'=16,'tp'=8] {'tp'}, dimensions={1} | all-to-all | bytes 524288 | tf_op jit(solution)/shard_map/all_to_all | solution.py:38
  35.1 3.4 all-to-all-start.1
  40.6 5.1 all-to-all-done.1
  46.6 29.8 %all-gather.3.cloned.1.call-done = bf16[16384,128]{1,0:T(8,128)(2,1)} async-done(((bf16[1024,128]{1,0:T(8,128)(2,1)}), bf16[16384,128]{1,0:T(8,128)(2,1)}) %all-gather.3.cloned.1.call-update) | async-done | bytes 4194320 | tf_op jit(solution)/shard_map/all_gather | solution.py:76
  76.4 55.5 %all-gather.5.cloned.1.call-done = bf16[16384,128]{1,0:T(8,128)(2,1)} async-done(((bf16[1024,128]{1,0:T(8,128)(2,1)}), bf16[16384,128]{1,0:T(8,128)(2,1)}) %all-gather.5.cloned.1.call-update) | async-done | bytes 4194320 | tf_op jit(solution)/shard_map/all_gather | solution.py:77
  132.0 6.6 %while.18 = (s32[]{:T(128)}, f32[1,1024]{1,0:T(1,128)S(1)}, f32[1,1024]{1,0:T(1,128)S(1)}, f32[1024,1,128]{0,2,1:T(8,128)S(1)}, s32[]{:T(128)}, /*index=5*/bf16[...) while((s32[]{:T(128)}, f32[1,1024]{1,0:T(1,128)S(1)}, ...), condition=%wide.region_5.6_spmd.clone, body=%wide.region_0.5_spmd.clone.sunk | while | flops 553914368 | bytes 14524729 | solution.py:92
  132.0 5.7 conditional.3
  141.5 4.4 all-to-all-start.3
  146.0 31.2 %all_gather.15 = bf16[128,2048]{1,0:T(8,128)(2,1)S(1)} all-gather(bf16[16,2048]{1,0:T(8,128)(2,1)S(1)} %convert_element_type.96), channel_id=1, replica_groups=mesh['seq'=16,'tp'=8] {'tp'}, dimensions={0}, use_global_device_ids=true | all-gather | bytes 589824 | tf_op jit(solution)/shard_map/all_gather | solution.py:125
  188.6 30.4 %all_gather.14 = bf16[128,2048]{1,0:T(8,128)(2,1)S(1)} all-gather(bf16[16,2048]{1,0:T(8,128)(2,1)S(1)} %multiply_convert_fusion.3), channel_id=1, replica_groups=mesh['seq'=16,'tp'=8] {'tp'}, dimensions={0}, use_global_device_ids=true | all-gather | bytes 589824 | tf_op jit(solution)/shard_map/all_gather | solution.py:106
  224.4 3.3 convolution_convert_fusion.3
  228.0 3.4 convolution_convert_fusion
  231.4 4.6 copy.35
  236.1 3.4 convolution_convert_fusion.1
  239.5 4.7 copy.33
  244.2 3.4 convolution_convert_fusion.2
  247.6 4.7 copy.37
  252.3 89.8 %reduce-scatter.14.cloned.1.call-done = bf16[16,2048]{1,0:T(8,128)(2,1)} async-done(((bf16[128,2048]{1,0:T(8,128)(2,1)}), bf16[16,2048]{1,0:T(8,128)(2,1)}) %reduce-scatter.14.cloned.1.call-update) | async-done | bytes 65552 | tf_op jit(solution)/shard_map/reduce_scatter | solution.py:131
  343.8 38.2 %reduce-scatter.12.cloned.1.call-done = bf16[16,2048]{1,0:T(8,128)(2,1)} async-done(((bf16[128,2048]{1,0:T(8,128)(2,1)}), bf16[16,2048]{1,0:T(8,128)(2,1)}) %reduce-scatter.12.cloned.1.call-update) | async-done | bytes 65552 | tf_op jit(solution)/shard_map/reduce_scatter | solution.py:111
  384.9 66.9 %psum.7 = f32[2048]{0:T(1024)} all-reduce(f32[2048]{0:T(1024)S(1)} %get-tuple-element.303), channel_id=1, replica_groups=mesh['seq'=16,'tp'=8] {'seq','tp'}, use_global_device_ids=true, to_apply=%region_16.17 | all-reduce | flops 2048 | bytes 16384 | tf_op jit(solution)/shard_map/psum | solution.py:144
  455.1 4.9 reduce-scatter.18.cloned.1.call-done
  461.8 76.1 %reduce-scatter.16.cloned.1.call-done = bf16[128,704]{1,0:T(8,128)(2,1)} async-done(((bf16[2048,704]{1,0:T(8,128)(2,1)}), bf16[128,704]{1,0:T(8,128)(2,1)}) %reduce-scatter.16.cloned.1.call-update) | async-done | bytes 180240
  539.7 76.3 %reduce-scatter.20.cloned.1.call-done = bf16[128,704]{1,0:T(8,128)(2,1)} async-done(((bf16[2048,704]{1,0:T(8,128)(2,1)}), bf16[128,704]{1,0:T(8,128)(2,1)}) %reduce-scatter.20.cloned.1.call-update) | async-done | bytes 180240
  (119 shorter events, 46.2 us)
Async XLA Ops:
  7.2 212.8 %copy-start = (bf16[2048,704]{0,1:T(8,128)(2,1)S(1)}, bf16[2048,704]{0,1:T(8,128)(2,1)}, u32[]{:S(2)}) copy-start(bf16[2048,704]{0,1:T(8,128)(2,1)} %param.20) | copy-start | bytes 8650756
  7.2 69.2 %all-gather.3.cloned.1.call-start = ((), (), s32[]{:S(2)}) async-start(), calls=%async_computation.9 | async-start | bytes 4456448 | tf_op jit(solution)/shard_map/all_gather | solution.py:76
  21.9 110.0 %all-gather.5.cloned.1.call-start = ((), (), s32[]{:S(2)}) async-start(), calls=%async_computation.10 | async-start | bytes 4456448 | tf_op jit(solution)/shard_map/all_gather | solution.py:77
  35.1 10.6 %all-to-all-start.1 = ((bf16[128,8,128]{0,2,1:T(8,128)(2,1)}), bf16[128,8,128]{0,2,1:T(8,128)(2,1)S(1)}, u32[]{:S(2)}, u32[]{:S(2)}) async-start(bf16[128,8,128]{0,2,1:T(8,128)(2,1)} %bitcast.10), calls=%async_computation.1 | async-start | bytes 524288 | tf_op jit(solution)/shard_map/all_to_all | solution.py:36
  40.0 0.6 copy-start.7
  141.5 35.7 %all-to-all-start.3 = ((bf16[8,128,128]{2,1,0:T(8,128)(2,1)}), bf16[8,128,128]{2,1,0:T(8,128)(2,1)}, u32[]{:S(2)}, u32[]{:S(2)}) async-start(bf16[8,128,128]{2,1,0:T(8,128)(2,1)} %bitcast.16), calls=%async_computation.3 | async-start | bytes 524288 | tf_op jit(solution)/shard_map/all_to_all | solution.py:96
  146.0 196.2 %reduce-scatter.14.cloned.1.call-start = ((), (), s32[]{:S(2)}) async-start(), calls=%async_computation.12 | async-start | bytes 589824 | tf_op jit(solution)/shard_map/reduce_scatter | solution.py:131
  177.2 9.1 %copy-start.5 = (bf16[128,2048]{1,0:T(8,128)(2,1)}, bf16[128,2048]{1,0:T(8,128)(2,1)S(1)}, u32[]{:S(2)}) copy-start(bf16[128,2048]{1,0:T(8,128)(2,1)S(1)} %all_gather.15) | copy-start | bytes 1572868
  179.2 6.2 copy-start.2
  179.2 8.9 %copy-start.10 = (f32[2048]{0:T(1024)S(1)}, f32[2048]{0:T(1024)}, u32[]{:S(2)}) copy-start(f32[2048]{0:T(1024)} %param.19) | copy-start | bytes 24580
  179.2 39.9 %copy-start.1 = (bf16[2048,704]{0,1:T(8,128)(2,1)S(1)}, bf16[2048,704]{0,1:T(8,128)(2,1)}, u32[]{:S(2)}) copy-start(bf16[2048,704]{0,1:T(8,128)(2,1)} %param.21) | copy-start | bytes 8650756
  182.4 37.5 %copy-start.3 = (bf16[128,2048]{1,0:T(8,128)(2,1)}, bf16[128,2048]{1,0:T(8,128)(2,1)S(1)}, u32[]{:S(2)}) copy-start(bf16[128,2048]{1,0:T(8,128)(2,1)S(1)} %fusion.23) | copy-start | bytes 1572868
  182.5 4.5 collective-permute-start
  188.0 0.6 copy-start.11
  221.6 0.7 copy-start.8
  221.6 1.3 copy-start.9
  224.3 157.6 %reduce-scatter.12.cloned.1.call-start = ((), (), s32[]{:S(2)}) async-start(), calls=%async_computation.11 | async-start | bytes 589824 | tf_op jit(solution)/shard_map/reduce_scatter | solution.py:111
  227.7 232.2 %reduce-scatter.18.cloned.1.call-start = ((), (), s32[]{:S(2)}) async-start(), calls=%async_computation.14 | async-start | bytes 3342336
  236.0 301.8 %reduce-scatter.16.cloned.1.call-start = ((), (), s32[]{:S(2)}) async-start(), calls=%async_computation.13 | async-start | bytes 3342336
  239.5 4.7 copy-start.6
  244.2 371.9 %reduce-scatter.20.cloned.1.call-start = ((), (), s32[]{:S(2)}) async-start(), calls=%async_computation.15 | async-start | bytes 3342336
  252.3 200.4 %copy-start.4 = (bf16[128,2048]{1,0:T(8,128)(2,1)S(1)}, bf16[128,2048]{1,0:T(8,128)(2,1)}, u32[]{:S(2)}) copy-start(bf16[128,2048]{1,0:T(8,128)(2,1)} %copy-done.3) | copy-start | bytes 1572868
  383.6 68.2 %collective-permute-start.1 = (f32[1,2048]{1,0:T(1,128)S(1)}, f32[1,2048]{1,0:T(1,128)}, u32[]{:S(2)}, u32[]{:S(2)}) collective-permute-start(f32[1,2048]{1,0:T(1,128)S(1)} %slice.27), channel_id=1, source_target_pairs={{1,0},{2,1},{3,2},{4,3},{5,4},{6,5},{7,6},{8,7},{9,8},{10,9},{11,1... | collective-permute-start | bytes 24584 | tf_op jit(solution)/shard_map/ppermute | solution.py:19
Sparse Core Ops, SparseCore 0:
  22.0 54.3 all-gather.2
  78.8 53.0 all-gather.4
  224.5 117.6 reduce-scatter.13
  345.1 36.8 reduce-scatter.11
  385.9 73.9 reduce-scatter.17
  463.8 73.9 reduce-scatter.15
  541.9 74.1 reduce-scatter.19
where the time goes:
time: 627 us; the launch traced here: 625 us
  waiting for transfers between devices  377 us (60%)
  blocking collectives  152 us (24%)
  local copies, waits for them, and re-layouts  27 us (4%)
  matrix products  26.4 us (4%)
  other arithmetic  14.7 us (2%)
  between operations  14.4 us (2%)
  starting transfers between devices  12.5 us (2%)
    unnamed x10, waiting for transfers between devices  157 us
    reduce_scatter x1, waiting for transfers between devices, on_device(): lax.psum_scatter((lax.dot_general(gate_delta, gate_weight, contract_last,...  89.8 us
    psum x1, blocking collectives, on_device(): gain_grad = lax.psum(jnp.sum(normed_grad * base, axis=0), ('seq', 'tp'))  66.9 us
    all_gather x1, waiting for transfers between devices, on_device(): value_piece = lax.all_gather(v_heads, 'seq', axis=0, tiled=True)  55.5 us
    reduce_scatter x1, waiting for transfers between devices, on_device(): lax.psum_scatter(jnp.dot(hidden, down_weight, preferred_element_type=jnp....  38.2 us
    all_gather x1, blocking collectives, on_device(): grad_group = lax.all_gather(coarse_grad_b, 'tp', axis=0, tiled=True)  31.2 us
    all_gather x1, blocking collectives, on_device(): normed_group = lax.all_gather(normed, 'tp', axis=0, tiled=True)  30.4 us
    all_gather x1, waiting for transfers between devices, on_device(): key_piece = lax.all_gather(k_heads, 'seq', axis=0, tiled=True)  29.8 us
  transfers between devices with their start and end apart: 11, of which 9 were waited for; matrix products, arithmetic and copies ran while one was open for 7% of the time, Pallas kernels for 0%

commit v1 on v0

--- a/solution.py
+++ b/solution.py
@@ -1,16 +1,314 @@
+import math
+
 import jax
 import jax.numpy as jnp
 from jax import lax
+from jax.experimental import pallas as pl
+from jax.experimental.pallas import tpu as pltpu
 from jax.sharding import PartitionSpec as P
 
 D = 2048
 HEAD = 128
 SHORTEN = 8
-
+MESH = pl.DeviceIdType.MESH
+TP = 8
 
 contract_last = (((1,), (1,)), ((), ()))
 contract_first = (((0,), (0,)), ((), ()))
 very_low = -1e30
+POWER = math.log2(math.e) * HEAD ** (-0.5)
+TILE = 256
+
+
+def places():
+    s, t = lax.axis_index("seq"), lax.axis_index("tp")
+    half, block = s // 8, lax.rem(s, 8)
+    y, core = block // 2, lax.rem(block, 2)
+    sib = half * 8 + y * 2 + (1 - core)
+    up = half * 8 + lax.rem(y + 1, 4) * 2 + core
+    down = half * 8 + lax.rem(y + 3, 4) * 2 + core
+    partner = (1 - half) * 8 + block
+    return s, t, half, block, y, core, sib, up, down, partner
+
+
+def attend_kernel(
+    q_ref, k_ref, v_ref, att_ref,
+    vt_src, q_own, q_far, k_all, vt_all, m_ref, l_ref, acc_ref, far_m, far_l, far_acc,
+    o_out, o_in, stat_out, stat_in, o_rows, att, send, recv, local_sem,
+):
+    s, t, half, block, y, core, sib, up, down, partner = places()
+    rows = q_ref.shape[0]
+
+    barrier = pltpu.get_barrier_semaphore()
+    peers = [(s, lax.rem(t + off, TP)) for off in range(1, TP)]
+    peers += [(sib, t), (up, t), (down, t), (partner, t)]
+    for peer in peers:
+        pl.semaphore_signal(barrier, inc=1, device_id=peer, device_id_type=MESH)
+    pl.semaphore_wait(barrier, len(peers))
+
+    def remote(kind, src, dst, device):
+        return pltpu.make_async_remote_copy(
+            src_ref=src, dst_ref=dst, send_sem=send.at[kind], recv_sem=recv.at[kind],
+            device_id=device, device_id_type=MESH,
+        )
+
+    def lanes(index):
+        return pl.ds(pl.multiple_of(index * HEAD, HEAD), HEAD)
+
+    def band(index):
+        return pl.ds(pl.multiple_of(index * rows, rows), rows)
+
+    q_copies, k_copies, v_copies = [], [], []
+    for off in range(1, TP):
+        peer = lax.rem(t + off, TP)
+        cp = remote(off - 1, q_ref.at[:, lanes(peer)], q_own.at[band(t), :], (s, peer))
+        cp.start()
+        q_copies.append(cp)
+    for off in range(1, TP):
+        peer = lax.rem(t + off, TP)
+        cp = remote(6 + off, k_ref.at[:, lanes(peer)], k_all.at[block, band(t), :], (s, peer))
+        cp.start()
+        k_copies.append(cp)
+    for h in range(TP):
+        vt_src[h] = v_ref[:, h * HEAD : (h + 1) * HEAD].astype(jnp.float32).T.astype(jnp.bfloat16)
+    for off in range(1, TP):
+        peer = lax.rem(t + off, TP)
+        cp = remote(13 + off, vt_src.at[peer], vt_all.at[block, :, band(t)], (s, peer))
+        cp.start()
+        v_copies.append(cp)
+    own = [
+        pltpu.make_async_copy(q_ref.at[:, lanes(t)], q_own.at[band(t), :], local_sem.at[0]),
+        pltpu.make_async_copy(k_ref.at[:, lanes(t)], k_all.at[block, band(t), :], local_sem.at[1]),
+        pltpu.make_async_copy(vt_src.at[t], vt_all.at[block, :, band(t)], local_sem.at[2]),
+    ]
+    for cp in own:
+        cp.start()
+
+    for ref, value in ((m_ref, very_low), (l_ref, 0.0), (acc_ref, 0.0),
+                       (far_m, very_low), (far_l, 0.0), (far_acc, 0.0)):
+        ref[...] = jnp.full(ref.shape, value, jnp.float32)
+
+    for cp in own:
+        cp.wait()
+    for cp in q_copies:
+        cp.wait_recv()
+    q_over = remote(35, q_own, q_far, (partner, t))
+
+    @pl.when(half == 1)
+    def _():
+        q_over.start()
+
+    k_mine, v_mine = k_all.at[block], vt_all.at[block]
+    gather = [
+        remote(21, k_mine, k_mine, (up, t)), remote(22, k_mine, k_mine, (down, t)),
+        remote(23, k_mine, k_mine, (sib, t)),
+        remote(24, v_mine, v_mine, (up, t)), remote(25, v_mine, v_mine, (down, t)),
+        remote(26, v_mine, v_mine, (sib, t)),
+    ]
+    for cp in k_copies:
+        cp.wait_recv()
+    for cp in gather[:3]:
+        cp.start()
+    for cp in v_copies:
+        cp.wait_recv()
+    for cp in gather[3:]:
+        cp.start()
+
+    def block_of(step):
+        j = step // 2
+        dy = j + (j // 2) * (5 - 2 * j)
+        return lax.rem(y + dy, 4) * 2 + lax.rem(core + step, 2)
+
+    def fold(q_all, m_all, l_all, acc_all, key_block, tile, diagonal):
+        span = pl.ds(pl.multiple_of(tile * (2 * TILE), 2 * TILE), 2 * TILE)
+        keys = k_all[key_block]
+        scores = [
+            lax.dot_general(
+                keys, q_all[pl.ds(pl.multiple_of((2 * tile + u) * TILE, TILE), TILE), :],
+                contract_last, preferred_element_type=jnp.float32,
+            )
+            for u in range(2)
+        ]
+        values = vt_all[key_block]
+        for u in range(2):
+            cols = pl.ds(pl.multiple_of((2 * tile + u) * TILE, TILE), TILE)
+            st = scores[u]
+            if diagonal:
+                key_pos = lax.broadcasted_iota(jnp.int32, st.shape, 0)
+                query_pos = lax.broadcasted_iota(jnp.int32, st.shape, 1) + (2 * tile + u) * TILE
+                st = jnp.where(key_pos <= query_pos, st, very_low)
+            before = m_all[:, cols]
+            fresh = jnp.maximum(before, jnp.max(st, axis=0, keepdims=True))
+            weights = jnp.exp2((st - fresh) * POWER)
+            factor = jnp.exp2((before - fresh) * POWER)
+            m_all[:, cols] = fresh
+            l_all[:, cols] = l_all[:, cols] * factor + jnp.sum(weights, axis=0, keepdims=True)
+            acc_all[:, cols] = acc_all[:, cols] * factor + jnp.dot(
+                values, weights.astype(jnp.bfloat16), preferred_element_type=jnp.float32
+            )
+
+    tiles = q_own.shape[0] // (2 * TILE)
+
+    def own_steps(first, last):
+        @pl.loop(first, last)
+        def _(step):
+            key_block = block_of(step)
+
+            @pl.when(key_block < block)
+            def _():
+                @pl.loop(0, tiles)
+                def _(tile):
+                    fold(q_own, m_ref, l_ref, acc_ref, key_block, tile, False)
+
+    def far_steps(first, last):
+        @pl.when(half == 0)
+        def _():
+            @pl.loop(first, last)
+            def _(step):
+                @pl.loop(0, tiles)
+                def _(tile):
+                    fold(q_far, far_m, far_l, far_acc, block_of(step), tile, False)
+
+    @pl.loop(0, tiles)
+    def _(tile):
+        fold(q_own, m_ref, l_ref, acc_ref, block, tile, True)
+
+    gather[2].wait_recv()
+    gather[5].wait_recv()
+
+    @pl.when(half == 0)
+    def _():
+        q_over.wait_recv()
+
+    far_steps(0, 2)
+    k_below, v_below = k_all.at[block_of(4)], vt_all.at[block_of(4)]
+    k_above, v_above = k_all.at[block_of(2)], vt_all.at[block_of(2)]
+    k_across, v_across = k_all.at[block_of(6)], vt_all.at[block_of(6)]
+    passed = [
+        remote(27, k_below, k_below, (up, t)), remote(28, v_above, v_above, (down, t)),
+        remote(29, k_above, k_above, (sib, t)), remote(30, v_above, v_above, (sib, t)),
+        remote(31, k_below, k_below, (sib, t)), remote(32, v_below, v_below, (sib, t)),
+        remote(33, k_across, k_across, (sib, t)), remote(34, v_across, v_across, (sib, t)),
+    ]
+    gather[0].wait_recv()
+    passed[0].start()
+    passed[4].start()
+    gather[1].wait_recv()
+    passed[2].start()
+    gather[4].wait_recv()
+    passed[1].start()
+    passed[3].start()
+    gather[3].wait_recv()
+    passed[5].start()
+    far_steps(2, 3)
+    for cp in passed[2:4]:
+        cp.wait_recv()
+    far_steps(3, 5)
+    for cp in passed[4:6]:
+        cp.wait_recv()
+    passed[0].wait_recv()
+    passed[6].start()
+    passed[1].wait_recv()
+    passed[7].start()
+    far_steps(5, 7)
+    for cp in passed[6:8]:
+        cp.wait_recv()
+    far_steps(7, 8)
+
+    o_over = remote(36, o_out, o_in, (partner, t))
+    stat_over = remote(37, stat_out, stat_in, (partner, t))
+
+    @pl.when(half == 0)
+    def _():
+        o_out[...] = (far_acc[...] / far_l[...]).astype(jnp.bfloat16)
+        stat_out[0:1] = far_m[...]
+        stat_out[1:2] = far_l[...]
+        o_over.start()
+        stat_over.start()
+        o_in[...] = jnp.zeros(o_in.shape, o_in.dtype)
+        stat_in[0:1] = jnp.full(far_m.shape, very_low, jnp.float32)
+        stat_in[1:2] = jnp.zeros(far_l.shape, jnp.float32)
+
+    own_steps(1, 8)
+
+    @pl.when(half == 1)
+    def _():
+        o_over.wait_recv()
+        stat_over.wait_recv()
+
+    other_m, other_l = stat_in[0:1], stat_in[1:2]
+    top = jnp.maximum(m_ref[...], other_m)
+    mine = jnp.exp2((m_ref[...] - top) * POWER)
+    other = other_l * jnp.exp2((other_m - top) * POWER)
+    total = l_ref[...] * mine + other
+    mine, other = mine / total, other / total
+    back = []
+    for h in range(TP):
+        cols = slice(h * rows, (h + 1) * rows)
+        mixed = acc_ref[:, cols] * mine[:, cols] + o_in[:, cols].astype(jnp.float32) * other[:, cols]
+        o_rows[h] = mixed.T.astype(jnp.bfloat16)
+    for off in range(1, TP):
+        peer = lax.rem(t + off, TP)
+        cp = remote(37 + off, o_rows.at[peer], att.at[:, lanes(t)], (s, peer))
+        cp.start()
+        back.append(cp)
+    own_back = pltpu.make_async_copy(o_rows.at[t], att.at[:, lanes(t)], local_sem.at[3])
+    own_back.start()
+    own_back.wait()
+    for cp in back:
+        cp.wait_recv()
+    att_ref[...] = att[...]
+
+    for cp in q_copies + k_copies + v_copies + gather + passed + back:
+        cp.wait_send()
+
+    @pl.when(half == 1)
+    def _():
+        q_over.wait_send()
+
+    @pl.when(half == 0)
+    def _():
+        o_over.wait_send()
+        stat_over.wait_send()
+
+
+def attention_of(queries, keys, values):
+    rows, width = queries.shape
+    group = rows * TP
+    f32, bf16 = jnp.float32, jnp.bfloat16
+    vmem = pl.BlockSpec(memory_space=pltpu.VMEM)
+    return pl.pallas_call(
+        attend_kernel,
+        out_shape=jax.ShapeDtypeStruct((rows, width), bf16),
+        in_specs=[vmem] * 3,
+        out_specs=vmem,
+        scratch_shapes=[
+            pltpu.VMEM((TP, HEAD, rows), bf16),
+            pltpu.VMEM((group, HEAD), bf16),
+            pltpu.VMEM((group, HEAD), bf16),
+            pltpu.VMEM((8, group, HEAD), bf16),
+            pltpu.VMEM((8, HEAD, group), bf16),
+            pltpu.VMEM((1, group), f32),
+            pltpu.VMEM((1, group), f32),
+            pltpu.VMEM((HEAD, group), f32),
+            pltpu.VMEM((1, group), f32),
+            pltpu.VMEM((1, group), f32),
+            pltpu.VMEM((HEAD, group), f32),
+            pltpu.VMEM((HEAD, group), bf16),
+            pltpu.VMEM((HEAD, group), bf16),
+            pltpu.VMEM((8, group), f32),
+            pltpu.VMEM((8, group), f32),
+            pltpu.VMEM((TP, rows, HEAD), bf16),
+            pltpu.VMEM((rows, width), bf16),
+            pltpu.SemaphoreType.DMA((45,)),
+            pltpu.SemaphoreType.DMA((45,)),
+            pltpu.SemaphoreType.DMA((4,)),
+        ],
+        compiler_params=pltpu.CompilerParams(
+            collective_id=0, has_side_effects=True, vmem_limit_bytes=48 * 1024 * 1024
+        ),
+        name="attention",
+    )(queries, keys, values)
 
 
 def shifted(value, axis, steps):
@@ -32,68 +330,7 @@
     cotangent,
 ):
     tok = fine_stream.shape[0]
-    q_heads, k_heads, v_heads = (
-        lax.all_to_all(queries, "tp", split_axis=1, concat_axis=0, tiled=True),
-        lax.all_to_all(keys, "tp", split_axis=1, concat_axis=0, tiled=True),
-        lax.all_to_all(values, "tp", split_axis=1, concat_axis=0, tiled=True),
-    )
-    group_rows = q_heads.shape[0]
-    heads_here = q_heads.shape[1] // HEAD
-    group_start = lax.axis_index("seq") * group_rows
-    query_pos = group_start + jnp.arange(group_rows, dtype=jnp.int32)
-    last_query = group_start + group_rows - 1
-    q_split = q_heads.reshape(group_rows, heads_here, HEAD)
-
-    def attend_block(carry, key_block, value_block, key_start):
-        maxima, totals, summed = carry
-        scores = jnp.einsum(
-            "qhd,khd->hqk",
-            q_split,
-            key_block.reshape(-1, heads_here, HEAD),
-            preferred_element_type=jnp.float32,
-        ) * HEAD ** (-0.5)
-        key_pos = key_start + jnp.arange(key_block.shape[0], dtype=jnp.int32)
-        visible = (query_pos[:, None] >= key_pos[None, :])[None]
-        masked = jnp.where(visible, scores, very_low)
-        fresh = jnp.maximum(maxima, jnp.max(masked, axis=-1))
-        weights = jnp.where(visible, jnp.exp(masked - fresh[..., None]), 0.0)
-        factor = jnp.exp(maxima - fresh)
-        totals = totals * factor + jnp.sum(weights, axis=-1)
-        mixed = jnp.einsum(
-            "hqk,khd->qhd",
-            weights.astype(jnp.bfloat16),
-            value_block.reshape(-1, heads_here, HEAD),
-            preferred_element_type=jnp.float32,
-        )
-        summed = summed * factor.T[..., None] + mixed
-        return (fresh, totals, summed)
-
-    initial = (
-        jnp.full((heads_here, group_rows), very_low, jnp.float32),
-        jnp.zeros((heads_here, group_rows), jnp.float32),
-        jnp.zeros((group_rows, heads_here, HEAD), jnp.float32),
-    )
-    key_piece = lax.all_gather(k_heads, "seq", axis=0, tiled=True)
-    value_piece = lax.all_gather(v_heads, "seq", axis=0, tiled=True)
-    width = min(group_rows, key_piece.shape[0])
-    blocks = key_piece.shape[0] // width
-
-    def one_block(index, inner):
-        offset = index * width
-        key_block = lax.dynamic_slice_in_dim(key_piece, offset, width, 0)
-        value_block = lax.dynamic_slice_in_dim(value_piece, offset, width, 0)
-        return lax.cond(
-            offset <= last_query,
-            lambda c: attend_block(c, key_block, value_block, offset),
-            lambda c: c,
-            inner,
-        )
-
-    maxima, totals, summed = lax.fori_loop(0, blocks, one_block, initial)
-    attn_heads = (
-        (summed / totals.T[..., None]).reshape(group_rows, heads_here * HEAD).astype(jnp.bfloat16)
-    )
-    attention = lax.all_to_all(attn_heads, "tp", split_axis=0, concat_axis=1, tiled=True)
+    attention = attention_of(queries, keys, values)
     projected = jnp.dot(attention, out_weight, preferred_element_type=jnp.float32)
     stream = (fine_stream.astype(jnp.float32) + projected).astype(jnp.bfloat16)
     crows = tok // SHORTEN

time: 627 us -> 464 us (0.74)
  waiting for transfers between devices: 377 us -> 212 us
  Pallas kernels: 0 us -> 51.8 us
  blocking collectives: 152 us -> 127 us
  starting transfers between devices: 12.5 us -> 5.24 us
    all_gather x2 -> x0, waiting for transfers between devices: 85.3 us -> none  [the longest x1 55.5 us: on_device(): value_piece = lax.all_gather(v_heads, 'seq', axis=0, tiled=True)]
    reduce_scatter x1, waiting for transfers between devices: 89.8 us -> 16.1 us  [on_device(): lax.psum_scatter((lax.dot_general(gate_delta, gate_weight, contract_last,...]
    pallas_call x0 -> x1, Pallas kernels: none -> 51.8 us  [attention_of(): pl.pallas_call(attend_kernel, out_shape=jax.ShapeDtypeStruct((rows, width...]
    all_to_all x2 -> x0, blocking collectives: 23.9 us -> none  [the longest x1 13.5 us: on_device(): lax.all_to_all(keys, 'tp', split_axis=1, concat_axis=0, tiled=True)]
    all_to_all x2 -> x0, starting transfers between devices: 7.85 us -> none  [the longest x1 4.43 us: on_device(): lax.all_to_all(attn_heads, 'tp', split_axis=0, concat_axis=1, tiled=True)]
    unnamed x31 -> x36, local copies, waits for them, and re-layouts: 20.8 us -> 21.5 us
    unnamed x10 -> x8, waiting for transfers between devices: 157 us -> 157 us
  transfers between devices with their start and end apart: 11 -> 7, of which waited for: 9 -> 5; matrix products, arithmetic and copies ran while one was open for 7% -> 8% of each run, Pallas kernels for 0% -> 0%
where the time goes in v1:
time: 464 us; the launch traced here: 463 us
  waiting for transfers between devices  212 us (46%)
  blocking collectives  127 us (27%)
  Pallas kernels  51.8 us (11%)
  matrix products  22.5 us (5%)
  local copies, waits for them, and re-layouts  21.6 us (5%)
  between operations  14 us (3%)
  other arithmetic  10.1 us (2%)
  starting transfers between devices  5.24 us (1%)
    unnamed x8, waiting for transfers between devices  157 us
    psum x1, blocking collectives, on_device(): gain_grad = lax.psum(jnp.sum(normed_grad * base, axis=0), ('seq', 'tp'))  67.2 us
    pallas_call x1, Pallas kernels, attention_of(): pl.pallas_call(attend_kernel, out_shape=jax.ShapeDtypeStruct((rows, width...  51.8 us
    reduce_scatter x1, waiting for transfers between devices, on_device(): lax.psum_scatter(jnp.dot(hidden, down_weight, preferred_element_type=jnp....  38.4 us
    all_gather x1, blocking collectives, on_device(): grad_group = lax.all_gather(coarse_grad_b, 'tp', axis=0, tiled=True)  29.8 us
    all_gather x1, blocking collectives, on_device(): normed_group = lax.all_gather(normed, 'tp', axis=0, tiled=True)  29.5 us
    unnamed x36, local copies, waits for them, and re-layouts  21.5 us
    reduce_scatter x1, waiting for transfers between devices, on_device(): lax.psum_scatter((lax.dot_general(gate_delta, gate_weight, contract_last,...  16.1 us
  transfers between devices with their start and end apart: 7, of which 5 were waited for; matrix products, arithmetic and copies ran while one was open for 8% of the time, Pallas kernels for 0%

profile of v1, /device:TPU:0, one launch (start us, length us, event | category | flops | bytes accessed | tf_op | source)
XLA Modules:
  0.0 463.5 jit_solution(7562931831633786862)
XLA Ops:
  7.2 1.1 copy-done.1
  10.2 51.8 %attention.1 = bf16[128,1024]{1,0:T(8,128)(2,1)S(1)} custom-call(bf16[128,1024]{1,0:T(8,128)(2,1)S(1)} %copy-done.1, bf16[128,1024]{1,0:T(8,128)(2,1)S(1)} %copy-done.2, bf16[128,1024]{1,0:T(8,128)(2,1)S(1)} %copy-done.3), custom_call_target="tpu_custom_call" | custom-call | tf_op jit(solution)/shard_map/attention/pallas_call | solution.py:280
  62.0 3.2 fusion.1
  65.2 3.7 collective-permute-start
  70.0 29.8 %all_gather.7 = bf16[128,2048]{1,0:T(8,128)(2,1)S(1)} all-gather(bf16[16,2048]{1,0:T(8,128)(2,1)S(1)} %convert_element_type.73), channel_id=1, replica_groups=mesh['seq'=16,'tp'=8] {'tp'}, dimensions={0}, use_global_device_ids=true | all-gather | bytes 589824 | tf_op jit(solution)/shard_map/all_gather | solution.py:362
  102.0 29.5 %all_gather.6 = bf16[128,2048]{1,0:T(8,128)(2,1)S(1)} all-gather(bf16[16,2048]{1,0:T(8,128)(2,1)S(1)} %multiply_convert_fusion.3), channel_id=1, replica_groups=mesh['seq'=16,'tp'=8] {'tp'}, dimensions={0}, use_global_device_ids=true | all-gather | bytes 589824 | tf_op jit(solution)/shard_map/all_gather | solution.py:343
  132.5 1.7 multiply_convert_fusion
  135.4 1.4 fusion
  136.9 3.3 convolution_convert_fusion.3
  140.3 3.6 convolution_convert_fusion.2
  144.0 4.6 copy.20
  148.6 3.5 convolution_convert_fusion
  152.1 4.6 copy.18
  156.8 3.4 convolution_convert_fusion.1
  160.1 4.7 %copy.16 = bf16[2048,704]{1,0:T(8,128)(2,1)} copy(bf16[2048,704]{0,1:T(8,128)(2,1)} %convolution_convert_fusion.1) | data formatting | bytes 5767168
  164.8 16.1 %reduce-scatter.14.cloned.1.call-done = bf16[16,2048]{1,0:T(8,128)(2,1)} async-done(((bf16[128,2048]{1,0:T(8,128)(2,1)}), bf16[16,2048]{1,0:T(8,128)(2,1)}) %reduce-scatter.14.cloned.1.call-update) | async-done | bytes 65552 | tf_op jit(solution)/shard_map/reduce_scatter | solution.py:368
  182.5 38.4 %reduce-scatter.12.cloned.1.call-done = bf16[16,2048]{1,0:T(8,128)(2,1)} async-done(((bf16[128,2048]{1,0:T(8,128)(2,1)}), bf16[16,2048]{1,0:T(8,128)(2,1)}) %reduce-scatter.12.cloned.1.call-update) | async-done | bytes 65552 | tf_op jit(solution)/shard_map/reduce_scatter | solution.py:348
  220.9 1.6 fusion.10
  222.6 1.3 collective-permute-start.1
  223.9 67.2 %psum.7 = f32[2048]{0:T(1024)} all-reduce(f32[2048]{0:T(1024)S(1)} %get-tuple-element.6), channel_id=1, replica_groups=mesh['seq'=16,'tp'=8] {'seq','tp'}, use_global_device_ids=true, to_apply=%region_10.0 | all-reduce | flops 2048 | bytes 16384 | tf_op jit(solution)/shard_map/psum | solution.py:381
  292.0 2.4 fusion.3
  294.3 4.7 %reduce-scatter.20.cloned.1.call-done = bf16[128,704]{1,0:T(8,128)(2,1)} async-done(((bf16[2048,704]{1,0:T(8,128)(2,1)}), bf16[128,704]{1,0:T(8,128)(2,1)}) %reduce-scatter.20.cloned.1.call-update) | async-done | bytes 180240
  300.9 76.1 %reduce-scatter.18.cloned.1.call-done = bf16[128,704]{1,0:T(8,128)(2,1)} async-done(((bf16[2048,704]{1,0:T(8,128)(2,1)}), bf16[128,704]{1,0:T(8,128)(2,1)}) %reduce-scatter.18.cloned.1.call-update) | async-done | bytes 180240
  378.9 76.2 %reduce-scatter.16.cloned.1.call-done = bf16[128,704]{1,0:T(8,128)(2,1)} async-done(((bf16[2048,704]{1,0:T(8,128)(2,1)}), bf16[128,704]{1,0:T(8,128)(2,1)}) %reduce-scatter.16.cloned.1.call-update) | async-done | bytes 180240
  (64 shorter events, 15.5 us)
Async XLA Ops:
  7.2 125.3 %copy-start = (bf16[2048,704]{0,1:T(8,128)(2,1)S(1)}, bf16[2048,704]{0,1:T(8,128)(2,1)}, u32[]{:S(2)}) copy-start(bf16[2048,704]{0,1:T(8,128)(2,1)} %param.16) | copy-start | bytes 8650756
  7.2 173.8 %reduce-scatter.14.cloned.1.call-start = ((), (), s32[]{:S(2)}) async-start(), calls=%async_computation.6 | async-start | bytes 589824 | tf_op jit(solution)/shard_map/reduce_scatter | solution.py:368
  7.2 1.1 copy-start.1
  8.3 0.9 copy-start.2
  9.3 0.9 copy-start.3
  62.0 7.0 %copy-start.9 = (bf16[128,2048]{1,0:T(8,128)(2,1)S(1)}, bf16[128,2048]{1,0:T(8,128)(2,1)}, u32[]{:S(2)}) copy-start(bf16[128,2048]{1,0:T(8,128)(2,1)} %param.19) | copy-start | bytes 1572868
  62.0 37.8 %copy-start.5 = (bf16[704,2048]{1,0:T(8,128)(2,1)S(1)}, bf16[704,2048]{1,0:T(8,128)(2,1)}, u32[]{:S(2)}) copy-start(bf16[704,2048]{1,0:T(8,128)(2,1)} %param.18) | copy-start | bytes 8650756
  65.2 36.0 %copy-start.6 = (bf16[128,2048]{1,0:T(8,128)(2,1)}, bf16[128,2048]{1,0:T(8,128)(2,1)S(1)}, u32[]{:S(2)}) copy-start(bf16[128,2048]{1,0:T(8,128)(2,1)S(1)} %fusion.1) | copy-start | bytes 1572868
  65.2 35.6 %collective-permute-start = (bf16[8,2048]{1,0:T(8,128)(2,1)S(1)}, bf16[8,2048]{1,0:T(8,128)(2,1)S(1)}, u32[]{:S(2)}, u32[]{:S(2)}) collective-permute-start(bf16[8,2048]{1,0:T(8,128)(2,1)S(1)} %slice.25), channel_id=1, source_target_pairs={{0,1},{1,2},{2,3},{3,4},{4,5},{5,6},{6,7},{7,8},{8,9},{9,10},{10,1... | collective-permute-start | bytes 98312 | tf_op jit(solution)/shard_map/ppermute | solution.py:317
  69.4 0.7 copy-start.10
  70.0 31.9 %copy-start.13 = (f32[2048]{0:T(1024)S(1)}, f32[2048]{0:T(1024)}, u32[]{:S(2)}) copy-start(f32[2048]{0:T(1024)} %param.15) | copy-start | bytes 24580
  70.0 61.5 %copy-start.4 = (bf16[2048,704]{0,1:T(8,128)(2,1)S(1)}, bf16[2048,704]{0,1:T(8,128)(2,1)}, u32[]{:S(2)}) copy-start(bf16[2048,704]{0,1:T(8,128)(2,1)} %param.17) | copy-start | bytes 8650756
  99.9 2.0 copy-start.8
  101.9 29.6 %copy-start.14 = (f32[16]{0:T(128)}, f32[16]{0:T(128)S(1)}, u32[]{:S(2)}) copy-start(f32[16]{0:T(128)S(1)} %get-tuple-element.14) | copy-start | bytes 196
  134.1 0.7 copy-start.11
  134.1 1.3 copy-start.12
  136.9 84.1 %reduce-scatter.12.cloned.1.call-start = ((), (), s32[]{:S(2)}) async-start(), calls=%async_computation.5 | async-start | bytes 589824 | tf_op jit(solution)/shard_map/reduce_scatter | solution.py:348
  140.3 158.8 %reduce-scatter.20.cloned.1.call-start = ((), (), s32[]{:S(2)}) async-start(), calls=%async_computation.9 | async-start | bytes 3342336
  148.6 228.4 %reduce-scatter.18.cloned.1.call-start = ((), (), s32[]{:S(2)}) async-start(), calls=%async_computation.8 | async-start | bytes 3342336
  156.7 298.4 %reduce-scatter.16.cloned.1.call-start = ((), (), s32[]{:S(2)}) async-start(), calls=%async_computation.7 | async-start | bytes 3342336
  164.8 127.2 %copy-start.7 = (bf16[128,2048]{1,0:T(8,128)(2,1)S(1)}, bf16[128,2048]{1,0:T(8,128)(2,1)}, u32[]{:S(2)}) copy-start(bf16[128,2048]{1,0:T(8,128)(2,1)} %copy-done.6) | copy-start | bytes 1572868
  222.6 68.6 %collective-permute-start.1 = (f32[1,2048]{1,0:T(1,128)S(1)}, f32[1,2048]{1,0:T(1,128)}, u32[]{:S(2)}, u32[]{:S(2)}) collective-permute-start(f32[1,2048]{1,0:T(1,128)S(1)} %slice.27), channel_id=1, source_target_pairs={{1,0},{2,1},{3,2},{4,3},{5,4},{6,5},{7,6},{8,7},{9,8},{10,9},{11,1... | collective-permute-start | bytes 24584 | tf_op jit(solution)/shard_map/ppermute | solution.py:317
Sparse Core Ops, SparseCore 0:
  137.0 43.9 reduce-scatter.13
  184.0 36.8 reduce-scatter.11
  225.0 74.0 reduce-scatter.19
  303.0 73.9 reduce-scatter.17
  380.9 74.1 reduce-scatter.15

commit v2 on v1

--- a/solution.py
+++ b/solution.py
@@ -311,10 +311,313 @@
     )(queries, keys, values)
 
 
-def shifted(value, axis, steps):
-    count = lax.axis_size(axis)
-    leading, last = (max(0, -steps), min(count, count - steps))
-    return lax.ppermute(value, axis, [(source, source + steps) for source in range(leading, last)])
+def section_kernel(
+    att_ref, fine_ref, cot_ref, gain_ref, out_hbm, gate_hbm, up_hbm, down_hbm,
+    section_ref, stream_grad_ref, gate_grad_ref, up_grad_ref, down_grad_ref, gain_grad_ref,
+    out_w, gate_w, up_w, down_w, stream, border, coarse_b, coarse_grad_b, ng, gg, hidden_grad,
+    ng_t, gg_t, ng_all, gg_all, hgu, down_out, down_in, norm_out, norm_in, follow_out, follow_in,
+    gain_out, gain_in, gain_mid, gain_half, gain_far_out, gain_far_in, term_out, term_in,
+    send, recv, local_sem,
+):
+    s, t, half, block, y, core, sib, up, down, partner = places()
+    f32, bf16 = jnp.float32, jnp.bfloat16
+    tok = fine_ref.shape[0]
+    crows = tok // SHORTEN
+    group = crows * TP
+    hid = gate_w.shape[1]
+    number = lax.axis_size("seq") * TP
+    flat = s * TP + t
+    after, before = lax.rem(flat + 1, number), lax.rem(flat + number - 1, number)
+    after, before = (after // TP, lax.rem(after, TP)), (before // TP, lax.rem(before, TP))
+
+    weights = [
+        pltpu.make_async_copy(src, dst, local_sem.at[i])
+        for i, (src, dst) in enumerate(
+            ((out_hbm, out_w), (down_hbm, down_w), (gate_hbm, gate_w), (up_hbm, up_w))
+        )
+    ]
+    for cp in weights:
+        cp.start()
+
+    barrier = pltpu.get_barrier_semaphore()
+    peers = [(s, lax.rem(t + off, TP)) for off in range(1, TP)]
+    peers += [(half * 8 + lax.rem(block + off, 8), t) for off in range(1, 8)]
+    peers += [(partner, t), after, before]
+    for peer in peers:
+        pl.semaphore_signal(barrier, inc=1, device_id=peer, device_id_type=MESH)
+    pl.semaphore_wait(barrier, len(peers))
+
+    used = []
+
+    def remote(src, dst, device):
+        kind = len(used)
+        cp = pltpu.make_async_remote_copy(
+            src_ref=src, dst_ref=dst, send_sem=send.at[kind], recv_sem=recv.at[kind],
+            device_id=device, device_id_type=MESH,
+        )
+        used.append(cp)
+        return cp
+
+    def go(copies):
+        for cp in copies:
+            cp.start()
+        return copies
+
+    def landed(copies):
+        for cp in copies:
+            cp.wait_recv()
+
+    def to_group(src, dst):
+        return go([
+            remote(src(lax.rem(t + off, TP)), dst, (s, lax.rem(t + off, TP))) for off in range(1, TP)
+        ])
+
+    def aligned(index, size):
+        return pl.ds(pl.multiple_of(index * size, size), size)
+
+    mine = aligned(t, crows)
+
+    row = lax.broadcasted_iota(jnp.int32, (crows, tok), 0)
+    col = lax.broadcasted_iota(jnp.int32, (crows, tok), 1)
+    members = jnp.where((col >= row * SHORTEN) & (col < row * SHORTEN + SHORTEN), 1.0, 0.0).astype(bf16)
+    coarse_grad = jnp.dot(members, cot_ref[...], preferred_element_type=f32)
+    coarse_grad_b[...] = coarse_grad.astype(bf16)
+    gg[mine, :] = coarse_grad_b[...]
+    grad_gather = to_group(lambda peer: coarse_grad_b, gg.at[mine, :])
+
+    weights[0].wait()
+    projected = jnp.dot(att_ref[...], out_w[...], preferred_element_type=f32)
+    stream[...] = (fine_ref[...].astype(f32) + projected).astype(bf16)
+    border_copy = remote(stream.at[pl.ds(tok - 16, 16), :], border, after)
+    border_copy.start()
+    window = jnp.where((col >= row * SHORTEN - (SHORTEN - 1)) & (col <= row * SHORTEN), 1.0, 0.0)
+    coarse = jnp.dot(window.astype(bf16), stream[...], preferred_element_type=f32)
+    edge_row = lax.broadcasted_iota(jnp.int32, (crows, 16), 0)
+    edge_col = lax.broadcasted_iota(jnp.int32, (crows, 16), 1)
+    edge = jnp.where((edge_row == 0) & (edge_col > 16 - SHORTEN) & (flat > 0), 1.0, 0.0)
+    border_copy.wait_recv()
+    coarse = coarse + jnp.dot(edge.astype(bf16), border[...], preferred_element_type=f32)
+    coarse = coarse / SHORTEN
+    rstd = lax.rsqrt(jnp.mean(coarse * coarse, axis=-1, keepdims=True) + 1e-05)
+    base = coarse * rstd
+    coarse_b[...] = (base * gain_ref[...]).astype(bf16)
+    ng[mine, :] = coarse_b[...]
+    norm_gather = to_group(lambda peer: coarse_b, ng.at[mine, :])
+
+    landed(grad_gather)
+    weights[1].wait()
+    hidden_grad[...] = lax.dot_general(
+        gg[...], down_w[...], contract_last, preferred_element_type=f32
+    )
+
+    def to_columns(rows_ref, turned, gathered, sem):
+        for i in range(turned.shape[0]):
+            turned[i] = rows_ref[:, i * HEAD : (i + 1) * HEAD].astype(f32).T.astype(bf16)
+        copies = []
+        for part in range(2):
+            dst = gathered.at[part, :, aligned(block, group)]
+            for off in range(1, 8):
+                peer = lax.rem(block + off, 8)
+                copies.append(remote(turned.at[part * 8 + peer], dst, (half * 8 + peer, t)))
+            kept = pltpu.make_async_copy(turned.at[part * 8 + block], dst, local_sem.at[sem + part])
+            kept.start()
+            kept.wait()
+        return go(copies)
+
+    grad_columns = to_columns(gg, gg_t, gg_all, 4)
+
+    landed(norm_gather)
+    weights[2].wait()
+    weights[3].wait()
+    gate = jnp.dot(ng[...], gate_w[...], preferred_element_type=f32)
+    up_v = jnp.dot(ng[...], up_w[...], preferred_element_type=f32)
+    sig = jax.nn.sigmoid(gate)
+    act = gate * sig
+    hgu[block, 0:group] = (act * up_v).astype(bf16)
+    hgu[block, group : 2 * group] = (
+        hidden_grad[...] * up_v * sig * (1.0 + gate * (1.0 - sig))
+    ).astype(bf16)
+    hgu[block, 2 * group : 3 * group] = (hidden_grad[...] * act).astype(bf16)
+
+    cut = 3 * group // 2
+    pieces = (pl.ds(0, cut), pl.ds(cut, cut))
+    above, below, across = (lax.rem(y + dy, 4) * 2 + core for dy in (1, 3, 2))
+
+    def ring(source, piece, device):
+        ref = hgu.at[source, pieces[piece], :]
+        return remote(ref, ref, (device, t))
+
+    ring_up = go([ring(block, 0, up), ring(block, 1, up)])
+    ring_down = go([ring(block, 1, down), ring(block, 0, down)])
+    ring_sib = go([ring(block, 0, sib), ring(block, 1, sib)])
+
+    part = jnp.dot(hgu[block, 0:group], down_w[...], preferred_element_type=f32)
+    down_out[...] = part.astype(bf16).reshape(down_out.shape)
+    down_in[t] = down_out[t]
+    down_sum = to_group(lambda peer: down_out.at[peer], down_in.at[t])
+    part = lax.dot_general(
+        hgu[block, group : 2 * group], gate_w[...], contract_last, preferred_element_type=f32
+    ) + lax.dot_general(
+        hgu[block, 2 * group : 3 * group], up_w[...], contract_last, preferred_element_type=f32
+    )
+    norm_out[...] = part.astype(bf16).reshape(norm_out.shape)
+    norm_in[t] = norm_out[t]
+    norm_sum = to_group(lambda peer: norm_out.at[peer], norm_in.at[t])
+    norm_columns = to_columns(ng, ng_t, ng_all, 6)
+
+    landed(ring_up[:1])
+    onward = go([ring(below, 0, up), ring(below, 0, sib)])
+    landed(ring_down[:1])
+    onward += go([ring(above, 1, down), ring(above, 1, sib)])
+    landed(ring_up[1:])
+    onward += go([ring(below, 1, sib)])
+    landed(ring_down[1:])
+    onward += go([ring(above, 0, sib)])
+
+    landed(down_sum)
+    coarse_out = coarse + jnp.sum(down_in[...].astype(f32), axis=0)
+    spread = (crows, SHORTEN, D)
+    section_ref[...] = (
+        (stream[...].astype(f32).reshape(spread) + coarse_out[:, None, :])
+        .reshape(tok, D)
+        .astype(bf16)
+    )
+
+    landed(norm_sum)
+    normed_grad = jnp.sum(norm_in[...].astype(f32), axis=0)
+    width = D // 8
+
+    def fold_row(ref, value):
+        for i in range(8):
+            ref[i : i + 1, :] = value[:, i * width : (i + 1) * width]
+
+    scaled = normed_grad * gain_ref[...]
+    coarse_total = coarse_grad + rstd * (
+        scaled - base * jnp.mean(scaled * base, axis=-1, keepdims=True)
+    )
+    fold_row(follow_out, coarse_total[0:1])
+    follow = remote(follow_out, follow_in, before)
+    follow.start()
+    fold_row(gain_out, jnp.sum(normed_grad * base, axis=0, keepdims=True))
+    gain_in[t] = gain_out[...]
+    gain_sum = to_group(lambda peer: gain_out, gain_in.at[t])
+
+    landed(onward[0:1] + onward[2:3])
+    last = go([ring(across, 0, sib), ring(across, 1, sib)])
+
+    follow.wait_recv()
+    following = jnp.concatenate([follow_in[i : i + 1, :] for i in range(8)], axis=1)
+    following = jnp.where(flat < number - 1, following, 0.0)
+    ahead = jnp.concatenate([coarse_total[1:], following], axis=0)
+    place = lax.broadcasted_iota(jnp.int32, spread, 1)
+    contrib = jnp.where(place == 0, coarse_total[:, None, :], ahead[:, None, :])
+    stream_grad_ref[...] = (
+        (cot_ref[...].astype(f32).reshape(spread) + contrib / SHORTEN).reshape(tok, D).astype(bf16)
+    )
+
+    landed(gain_sum)
+    gain_mid[...] = jnp.sum(gain_in[...], axis=0)
+    gain_half[block] = gain_mid[...]
+    gain_group = go([
+        remote(gain_mid, gain_half.at[block], (half * 8 + lax.rem(block + off, 8), t))
+        for off in range(1, 8)
+    ])
+
+    landed(ring_sib + onward[1:2] + onward[3:] + grad_columns + norm_columns + last)
+    outs = (down_grad_ref, gate_grad_ref, up_grad_ref)
+
+    def term(i, part):
+        left = (gg_all if i == 0 else ng_all)[part]
+        right = hgu[:, i * group : (i + 1) * group, :].reshape(8 * group, hid)
+        return jnp.dot(left, right, preferred_element_type=f32)
+
+    terms = []
+    for i in range(3):
+        term_out[i] = term(i, 1 - half).astype(bf16)
+        terms += go([remote(term_out.at[i], term_in.at[i], (partner, t))])
+    landed(gain_group)
+    gain_far_out[...] = jnp.sum(gain_half[...], axis=0)
+    gain_far = remote(gain_far_out, gain_far_in, (partner, t))
+    gain_far.start()
+    for i in range(3):
+        outs[i][...] = term(i, half)
+    gain_far.wait_recv()
+    gain_grad_ref[...] = gain_far_out[...] + gain_far_in[...]
+    for i in range(3):
+        terms[i].wait_recv()
+        outs[i][...] = outs[i][...] + term_in[i].astype(f32)
+
+    for cp in used:
+        cp.wait_send()
+
+
+COPIES = 90
+
+
+def section_of(attention, fine_stream, cotangent, norm_gain, out_weight, gate_weight, up_weight, down_weight):
+    tok = fine_stream.shape[0]
+    crows = tok // SHORTEN
+    group = crows * TP
+    hid = gate_weight.shape[1]
+    seq = lax.axis_size("seq")
+    f32, bf16 = jnp.float32, jnp.bfloat16
+    vmem, anywhere = pl.BlockSpec(memory_space=pltpu.VMEM), pl.BlockSpec(memory_space=pl.ANY)
+    small = (8, D // 8)
+    return pl.pallas_call(
+        section_kernel,
+        out_shape=(
+            jax.ShapeDtypeStruct((tok, D), bf16),
+            jax.ShapeDtypeStruct((tok, D), bf16),
+            jax.ShapeDtypeStruct((D // seq, hid), f32),
+            jax.ShapeDtypeStruct((D // seq, hid), f32),
+            jax.ShapeDtypeStruct((D // seq, hid), f32),
+            jax.ShapeDtypeStruct(small, f32),
+        ),
+        in_specs=[vmem] * 4 + [anywhere] * 4,
+        out_specs=(vmem,) * 6,
+        scratch_shapes=[
+            pltpu.VMEM(out_weight.shape, bf16),
+            pltpu.VMEM(gate_weight.shape, bf16),
+            pltpu.VMEM(up_weight.shape, bf16),
+            pltpu.VMEM(down_weight.shape, bf16),
+            pltpu.VMEM((tok, D), bf16),
+            pltpu.VMEM((16, D), bf16),
+            pltpu.VMEM((crows, D), bf16),
+            pltpu.VMEM((crows, D), bf16),
+            pltpu.VMEM((group, D), bf16),
+            pltpu.VMEM((group, D), bf16),
+            pltpu.VMEM((group, hid), f32),
+            pltpu.VMEM((seq, HEAD, group), bf16),
+            pltpu.VMEM((seq, HEAD, group), bf16),
+            pltpu.VMEM((2, HEAD, 8 * group), bf16),
+            pltpu.VMEM((2, HEAD, 8 * group), bf16),
+            pltpu.VMEM((8, 3 * group, hid), bf16),
+            pltpu.VMEM((TP, crows, D), bf16),
+            pltpu.VMEM((TP, crows, D), bf16),
+            pltpu.VMEM((TP, crows, D), bf16),
+            pltpu.VMEM((TP, crows, D), bf16),
+            pltpu.VMEM(small, f32),
+            pltpu.VMEM(small, f32),
+            pltpu.VMEM(small, f32),
+            pltpu.VMEM((TP,) + small, f32),
+            pltpu.VMEM(small, f32),
+            pltpu.VMEM((8,) + small, f32),
+            pltpu.VMEM(small, f32),
+            pltpu.VMEM(small, f32),
+            pltpu.VMEM((3, HEAD, hid), bf16),
+            pltpu.VMEM((3, HEAD, hid), bf16),
+            pltpu.SemaphoreType.DMA((COPIES,)),
+            pltpu.SemaphoreType.DMA((COPIES,)),
+            pltpu.SemaphoreType.DMA((8,)),
+        ],
+        compiler_params=pltpu.CompilerParams(
+            collective_id=1, has_side_effects=True, vmem_limit_bytes=56 * 1024 * 1024
+        ),
+        name="section",
+    )(
+        attention, fine_stream, cotangent, norm_gain.reshape(1, D),
+        out_weight, gate_weight, up_weight, down_weight,
+    )
 
 
 def on_device(
@@ -329,86 +632,11 @@
     down_weight,
     cotangent,
 ):
-    tok = fine_stream.shape[0]
     attention = attention_of(queries, keys, values)
-    projected = jnp.dot(attention, out_weight, preferred_element_type=jnp.float32)
-    stream = (fine_stream.astype(jnp.float32) + projected).astype(jnp.bfloat16)
-    crows = tok // SHORTEN
-    border = shifted(stream[tok - SHORTEN :], ("seq", "tp"), 1)
-    extended = jnp.concatenate([border[1:], stream], 0)[:tok]
-    coarse = extended.astype(jnp.float32).reshape(crows, SHORTEN, D).sum(1) / SHORTEN
-    rstd = lax.rsqrt(jnp.mean(coarse * coarse, axis=-1, keepdims=True) + 1e-05)
-    base = coarse * rstd
-    normed = (base * norm_gain).astype(jnp.bfloat16)
-    normed_group = lax.all_gather(normed, "tp", axis=0, tiled=True)
-    gate = jnp.dot(normed_group, gate_weight, preferred_element_type=jnp.float32)
-    up = jnp.dot(normed_group, up_weight, preferred_element_type=jnp.float32)
-    sig = jax.nn.sigmoid(gate)
-    hidden = (gate * sig * up).astype(jnp.bfloat16)
-    coarse_out = coarse + lax.psum_scatter(
-        jnp.dot(hidden, down_weight, preferred_element_type=jnp.float32).astype(jnp.bfloat16),
-        "tp",
-        scatter_dimension=0,
-        tiled=True,
-    ).astype(jnp.float32)
-    section_out = (
-        (stream.astype(jnp.float32).reshape(crows, SHORTEN, D) + coarse_out[:, None, :])
-        .reshape(tok, D)
-        .astype(jnp.bfloat16)
-    )
-    grad = cotangent.astype(jnp.float32)
-    coarse_grad = grad.reshape(crows, SHORTEN, D).sum(1)
-    coarse_grad_b = coarse_grad.astype(jnp.bfloat16)
-    grad_group = lax.all_gather(coarse_grad_b, "tp", axis=0, tiled=True)
-    hidden_grad = lax.dot_general(
-        grad_group, down_weight, contract_last, preferred_element_type=jnp.float32
-    )
-    gate_delta = (hidden_grad * up * sig * (1.0 + gate * (1.0 - sig))).astype(jnp.bfloat16)
-    up_delta = (hidden_grad * gate * sig).astype(jnp.bfloat16)
-    normed_grad = lax.psum_scatter(
-        (
-            lax.dot_general(
-                gate_delta, gate_weight, contract_last, preferred_element_type=jnp.float32
-            )
-            + lax.dot_general(
-                up_delta, up_weight, contract_last, preferred_element_type=jnp.float32
-            )
-        ).astype(jnp.bfloat16),
-        "tp",
-        scatter_dimension=0,
-        tiled=True,
-    ).astype(jnp.float32)
-    gain_grad = lax.psum(jnp.sum(normed_grad * base, axis=0), ("seq", "tp"))
-    scaled = normed_grad * norm_gain
-    coarse_total = coarse_grad + rstd * (
-        scaled - base * jnp.mean(scaled * base, axis=-1, keepdims=True)
-    )
-    following = shifted(coarse_total[:1], ("seq", "tp"), -1)
-    ahead = jnp.concatenate([coarse_total[1:], following], 0)
-    spread = jnp.broadcast_to(ahead[:, None, :], (crows, SHORTEN, D)).reshape(tok, D)
-    contrib = jnp.concatenate([coarse_total[:1], spread[: tok - 1]], 0)
-    stream_grad = (grad + contrib / SHORTEN).astype(jnp.bfloat16)
-    gate_local = lax.dot_general(
-        normed_group, gate_delta, contract_first, preferred_element_type=jnp.float32
-    )
-    up_local = lax.dot_general(
-        normed_group, up_delta, contract_first, preferred_element_type=jnp.float32
-    )
-    gate_grad, up_grad = (
-        lax.psum_scatter(
-            gate_local.astype(jnp.bfloat16), "seq", scatter_dimension=0, tiled=True
-        ).astype(jnp.float32),
-        lax.psum_scatter(
-            up_local.astype(jnp.bfloat16), "seq", scatter_dimension=0, tiled=True
-        ).astype(jnp.float32),
-    )
-    down_local = lax.dot_general(
-        hidden, grad_group, contract_first, preferred_element_type=jnp.float32
-    )
-    down_grad = lax.psum_scatter(
-        down_local.astype(jnp.bfloat16), "seq", scatter_dimension=1, tiled=True
-    ).astype(jnp.float32)
-    return (section_out, stream_grad, gate_grad, up_grad, down_grad, gain_grad)
+    section_out, stream_grad, gate_grad, up_grad, down_grad, gain_grad = section_of(
+        attention, fine_stream, cotangent, norm_gain, out_weight, gate_weight, up_weight, down_weight
+    )
+    return (section_out, stream_grad, gate_grad, up_grad, down_grad.T, gain_grad.reshape(D))
 
 
 def solution(mesh):

time: 464 us -> 153 us (0.33)
  waiting for transfers between devices: 212 us -> 0 us
  blocking collectives: 127 us -> 0 us
  Pallas kernels: 51.8 us -> 130 us
  matrix products: 22.5 us -> 0 us
  between operations: 14 us -> 0.68 us
  other arithmetic: 10.1 us -> 0 us
  starting transfers between devices: 5.24 us -> 0 us
    unnamed x8 -> x0, waiting for transfers between devices: 157 us -> none
    pallas_call x0 -> x1, Pallas kernels: none -> 77.9 us  [section_of(): pl.pallas_call(section_kernel, out_shape=(jax.ShapeDtypeStruct((tok, D),...]
    psum x1 -> x0, blocking collectives: 67.2 us -> none  [on_device(): gain_grad = lax.psum(jnp.sum(normed_grad * base, axis=0), ('seq', 'tp'))]
    all_gather x2 -> x0, blocking collectives: 59.4 us -> none  [the longest x1 29.8 us: on_device(): grad_group = lax.all_gather(coarse_grad_b, 'tp', axis=0, tiled=True)]
    reduce_scatter x2 -> x0, waiting for transfers between devices: 54.5 us -> none  [the longest x1 38.4 us: on_device(): lax.psum_scatter(jnp.dot(hidden, down_weight, preferred_element_type=jnp....]
    dot_general x10 -> x0, matrix products: 22.5 us -> none  [the longest x1 3.64 us: on_device(): lax.dot_general(hidden, grad_group, contract_first, preferred_element_typ...]
    ppermute x2 -> x0, starting transfers between devices: 5.03 us -> none  [shifted(): lax.ppermute(value, axis, [(source, source + steps) for source in range(l...]
    convert_element_type x6 -> x0, other arithmetic: 4.76 us -> none  [the longest x1 2.36 us: on_device(): stream_grad = (grad + contrib / SHORTEN).astype(jnp.bfloat16)]
  transfers between devices with their start and end apart: 7 -> 0, of which waited for: 5 -> 0; matrix products, arithmetic and copies ran while one was open for 8% -> 0% of each run, Pallas kernels for 0% -> 0%
where the time goes in v2:
time: 153 us; the launch traced here: 151 us
  Pallas kernels  130 us (85%)
  local copies, waits for them, and re-layouts  20.8 us (14%)
    pallas_call x1, Pallas kernels, section_of(): pl.pallas_call(section_kernel, out_shape=(jax.ShapeDtypeStruct((tok, D),...  77.9 us
    pallas_call x1, Pallas kernels, attention_of(): pl.pallas_call(attend_kernel, out_shape=jax.ShapeDtypeStruct((rows, width...  51.8 us
    unnamed x20, local copies, waits for them, and re-layouts  20.8 us

profile of v2, /device:TPU:0, one launch (start us, length us, event | category | flops | bytes accessed | tf_op | source)
XLA Modules:
  0.0 151.1 jit_solution(2822669983100985877)
XLA Ops:
  0.6 0.0 copy-start.1
  0.6 0.9 copy-done.1
  1.6 0.0 copy-start.2
  1.6 0.9 copy-done.2
  2.5 0.0 copy-start.3
  2.5 0.9 copy-done.3
  3.5 51.8 %attention.1.att_ref = bf16[128,1024]{1,0:T(8,128)(2,1)S(1)} custom-call(bf16[128,1024]{1,0:T(8,128)(2,1)S(1)} %copy-done.1, bf16[128,1024]{1,0:T(8,128)(2,1)S(1)} %copy-done.2, bf16[128,1024]{1,0:T(8,128)(2,1)S(1)} %copy-done.3), custom_call_target="tpu_custom_call" | custom-call | tf_op jit(solution)/shard_map/attention/pallas_call | solution.py:280
  55.3 0.0 copy-start
  55.3 0.7 copy-done
  56.0 0.0 copy-start.4
  56.0 4.8 %copy.16.gate_hbm = bf16[2048,704]{1,0:T(8,128)(2,1)} copy(bf16[2048,704]{0,1:T(8,128)(2,1)} %param.16) | data formatting | bytes 5767168 | tf_op args[6]
  60.7 0.0 copy-done.4
  60.7 2.8 %copy.17.up_hbm = bf16[2048,704]{1,0:T(8,128)(2,1)} copy(bf16[2048,704]{0,1:T(8,128)(2,1)S(1)} %copy-done.4) | data formatting | bytes 5767168 | tf_op args[7]
  63.5 77.9 %section.1 = (bf16[128,2048]{1,0:T(8,128)(2,1)}, bf16[128,2048]{1,0:T(8,128)(2,1)}, f32[128,704]{1,0:T(8,128)}, f32[128,704]{1,0:T(8,128)}, f32[128,704]{1,0:T(8,128)}, /*index=5*/f32[8,256]{1,0:T(8,128)}) custom-call(bf16[128,1024]{1,0:T(8,128)(2,1)} %copy-done, bf16[128,2048]{1,0:T(8,128)(2,1)} %fine_ref.1, bf16[128,2048]{1,0:T(8,128)(2,1)} %cot_ref.1, ...), custom_call_target="tpu_custom_call" | custom-call | tf_op jit(solution)/shard_map/section/pallas_call | solution.py:566
  141.4 0.0 copy-start.5
  141.4 1.4 copy.21
  142.8 1.9 %copy.18 = f32[128,704]{0,1:T(8,128)} copy(f32[128,704]{1,0:T(8,128)} %get-tuple-element.20) | data formatting | bytes 720896
  144.7 1.9 %copy.19 = f32[128,704]{0,1:T(8,128)} copy(f32[128,704]{1,0:T(8,128)} %get-tuple-element.21) | data formatting | bytes 720896
  146.6 1.9 %copy.20 = f32[704,128]{1,0:T(8,128)} copy(f32[704,128]{0,1:T(8,128)} %bitcast.4) | data formatting | bytes 720896
  148.5 1.9 %copy.24 = bf16[128,2048]{1,0:T(8,128)(2,1)} copy(bf16[128,2048]{1,0:T(8,128)(2,1)} %get-tuple-element.30) | data formatting | bytes 1048576
  150.3 0.0 copy-done.5
  150.3 0.8 copy.25
Async XLA Ops:
  0.6 1.0 copy-start.1
  1.6 0.9 copy-start.2
  2.5 0.9 copy-start.3
  55.3 0.7 copy-start
  56.0 4.8 %copy-start.4 = (bf16[2048,704]{0,1:T(8,128)(2,1)S(1)}, bf16[2048,704]{0,1:T(8,128)(2,1)}, u32[]{:S(2)}) copy-start(bf16[2048,704]{0,1:T(8,128)(2,1)} %param.17) | copy-start | bytes 8650756
  141.4 8.9 %copy-start.5 = (bf16[128,2048]{1,0:T(8,128)(2,1)S(1)}, bf16[128,2048]{1,0:T(8,128)(2,1)}, u32[]{:S(2)}) copy-start(bf16[128,2048]{1,0:T(8,128)(2,1)} %get-tuple-element.31) | copy-start | bytes 1572868

commit v3 on v0

v3 whole, which is shorter than its diff:
```python
import math

import jax
import jax.numpy as jnp
from jax import lax
from jax.experimental import pallas as pl
from jax.experimental.pallas import tpu as pltpu
from jax.sharding import PartitionSpec as P

D = 2048
HEAD = 128
SHORTEN = 8
MESH = pl.DeviceIdType.MESH
TP = 8
WIDE = 512
COPIES = 160

contract_last = (((1,), (1,)), ((), ()))
contract_first = (((0,), (0,)), ((), ()))
very_low = -1e30
POWER = math.log2(math.e) * HEAD ** (-0.5)


def scratch_of(tok, hid, seq):
    crows, group, rows = tok // SHORTEN, tok // SHORTEN * TP, tok * TP
    f32, bf16 = jnp.float32, jnp.bfloat16
    vmem = pltpu.VMEM
    small = (8, D // 8)
    return {
        "q_in": vmem((tok, TP * HEAD), bf16),
        "k_in": vmem((tok, TP * HEAD), bf16),
        "v_in": vmem((tok, TP * HEAD), bf16),
        "fine": vmem((tok, D), bf16),
        "cot": vmem((tok, D), bf16),
        "out_w": vmem((TP * HEAD, D), bf16),
        "gate_w": vmem((hid, D), bf16),
        "up_w": vmem((hid, D), bf16),
        "down_w": vmem((hid, D), bf16),
        "vt_src": vmem((TP, HEAD, tok), bf16),
        "q_own": vmem((rows, HEAD), bf16),
        "q_far": vmem((rows, HEAD), bf16),
        "k_all": vmem((8, rows, HEAD), bf16),
        "vt_all": vmem((8, HEAD, rows), bf16),
        "scores": vmem((2, WIDE, WIDE), f32),
        "tops": vmem((2, 1, WIDE), f32),
        "m_own": vmem((1, rows), f32),
        "l_own": vmem((1, rows), f32),
        "acc_own": vmem((HEAD, rows), f32),
        "m_far": vmem((1, rows), f32),
        "l_far": vmem((1, rows), f32),
        "acc_far": vmem((HEAD, rows), f32),
        "o_out": vmem((HEAD, rows), bf16),
        "o_in": vmem((HEAD, rows), bf16),
        "stat_out": vmem((8, rows), f32),
        "stat_in": vmem((8, rows), f32),
        "o_rows": vmem((TP, tok, HEAD), bf16),
        "att": vmem((tok, TP * HEAD), bf16),
        "stream": vmem((tok, D), bf16),
        "border": vmem((16, D), bf16),
        "coarse_b": vmem((crows, D), bf16),
        "coarse_grad": vmem((crows, D), f32),
        "coarse_grad_b": vmem((crows, D), bf16),
        "ng": vmem((group, D), bf16),
        "gg": vmem((group, D), bf16),
        "hidden_grad": vmem((group, hid), f32),
        "ng_all": vmem((2, 8 * group, HEAD), bf16),
        "gg_all": vmem((2, 8 * group, HEAD), bf16),
        "hgu": vmem((3, 8, group, hid), bf16),
        "down_out": vmem((TP, crows, D), bf16),
        "down_in": vmem((TP, crows, D), bf16),
        "norm_out": vmem((TP, crows, D), bf16),
        "norm_in": vmem((TP, crows, D), bf16),
        "follow_out": vmem(small, f32),
        "follow_in": vmem(small, f32),
        "gain_out": vmem(small, f32),
        "gain_in": vmem((TP,) + small, f32),
        "gain_mid": vmem(small, f32),
        "gain_half": vmem((8,) + small, f32),
        "gain_far_out": vmem(small, f32),
        "gain_far_in": vmem(small, f32),
        "term_out": vmem((3, hid, HEAD), bf16),
        "term_in": vmem((3, hid, HEAD), bf16),
        "send": pltpu.SemaphoreType.DMA((COPIES,)),
        "recv": pltpu.SemaphoreType.DMA((COPIES,)),
        "local": pltpu.SemaphoreType.DMA((20,)),
    }


class Space:
    pass


def section_kernel(
    names, q_hbm, k_hbm, v_hbm, fine_hbm, cot_hbm, gain_ref, out_hbm, gate_hbm, up_hbm, down_hbm,
    section_ref, stream_grad_ref, gate_grad_ref, up_grad_ref, down_grad_ref, gain_grad_ref, *scratch,
):
    r = Space()
    for name, ref in zip(names, scratch):
        setattr(r, name, ref)
    f32, bf16 = jnp.float32, jnp.bfloat16
    s, t = lax.axis_index("seq"), lax.axis_index("tp")
    half, block = s // 8, lax.rem(s, 8)
    y, core = block // 2, lax.rem(block, 2)
    sib = half * 8 + y * 2 + (1 - core)
    up = half * 8 + lax.rem(y + 1, 4) * 2 + core
    down = half * 8 + lax.rem(y + 3, 4) * 2 + core
    partner = (1 - half) * 8 + block
    number = lax.axis_size("seq") * TP
    flat = s * TP + t
    after, before = lax.rem(flat + 1, number), lax.rem(flat + number - 1, number)
    after, before = (after // TP, lax.rem(after, TP)), (before // TP, lax.rem(before, TP))
    tok = r.fine.shape[0]
    crows = tok // SHORTEN
    group = crows * TP
    hid = r.gate_w.shape[0]

    loads = {}
    for name, src in (
        ("k_in", k_hbm), ("v_in", v_hbm), ("q_in", q_hbm), ("cot", cot_hbm), ("fine", fine_hbm),
        ("out_w", out_hbm), ("down_w", down_hbm), ("gate_w", gate_hbm), ("up_w", up_hbm),
    ):
        loads[name] = pltpu.make_async_copy(src, getattr(r, name), r.local.at[len(loads)])
        loads[name].start()

    barrier = pltpu.get_barrier_semaphore()
    peers = [(s, lax.rem(t + off, TP)) for off in range(1, TP)]
    peers += [(half * 8 + lax.rem(block + off, 8), t) for off in range(1, 8)]
    peers += [(partner, t), after, before]
    for peer in peers:
        pl.semaphore_signal(barrier, inc=1, device_id=peer, device_id_type=MESH)
    for ref, value in ((r.m_own, very_low), (r.l_own, 0.0), (r.acc_own, 0.0),
                       (r.m_far, very_low), (r.l_far, 0.0), (r.acc_far, 0.0)):
        ref[...] = jnp.full(ref.shape, value, f32)
    loads["v_in"].wait()
    for h in range(TP):
        r.vt_src[h] = r.v_in[:, h * HEAD : (h + 1) * HEAD].astype(f32).T.astype(bf16)
    loads["k_in"].wait()
    loads["q_in"].wait()
    pl.semaphore_wait(barrier, len(peers))

    used, sometimes = [], []

    def remote(src, dst, device, always=True):
        kind = len(used) + len(sometimes)
        cp = pltpu.make_async_remote_copy(
            src_ref=src, dst_ref=dst, send_sem=r.send.at[kind], recv_sem=r.recv.at[kind],
            device_id=device, device_id_type=MESH,
        )
        (used if always else sometimes).append(cp)
        return cp

    def go(copies):
        for cp in copies:
            cp.start()
        return copies

    def landed(copies):
        for cp in copies:
            cp.wait_recv()

    def to_group(src, dst):
        return go([
            remote(src(lax.rem(t + off, TP)), dst, (s, lax.rem(t + off, TP))) for off in range(1, TP)
        ])

    def aligned(index, size):
        return pl.ds(pl.multiple_of(index * size, size), size)

    def lanes(index):
        return aligned(index, HEAD)

    band = aligned(t, tok)
    k_copies = to_group(lambda peer: r.k_in.at[:, lanes(peer)], r.k_all.at[block, band, :])
    v_copies = to_group(lambda peer: r.vt_src.at[peer], r.vt_all.at[block, :, band])
    q_copies = to_group(lambda peer: r.q_in.at[:, lanes(peer)], r.q_own.at[band, :])
    own = go([
        pltpu.make_async_copy(r.q_in.at[:, lanes(t)], r.q_own.at[band, :], r.local.at[9]),
        pltpu.make_async_copy(r.k_in.at[:, lanes(t)], r.k_all.at[block, band, :], r.local.at[10]),
        pltpu.make_async_copy(r.vt_src.at[t], r.vt_all.at[block, :, band], r.local.at[11]),
    ])

    mine = aligned(t, crows)
    row = lax.broadcasted_iota(jnp.int32, (crows, tok), 0)
    col = lax.broadcasted_iota(jnp.int32, (crows, tok), 1)
    members = jnp.where((col >= row * SHORTEN) & (col < row * SHORTEN + SHORTEN), 1.0, 0.0).astype(bf16)
    loads["cot"].wait()
    r.coarse_grad[...] = jnp.dot(members, r.cot[...], preferred_element_type=f32)
    r.coarse_grad_b[...] = r.coarse_grad[...].astype(bf16)
    r.gg[mine, :] = r.coarse_grad_b[...]

    for cp in own:
        cp.wait()
    k_mine, v_mine = r.k_all.at[block], r.vt_all.at[block]
    landed(k_copies)
    k_ring = go([remote(k_mine, k_mine, (device, t)) for device in (up, down, sib)])
    landed(v_copies)
    v_ring = go([remote(v_mine, v_mine, (device, t)) for device in (down, up, sib)])
    landed(q_copies)
    q_over = remote(r.q_own, r.q_far, (partner, t), always=False)

    @pl.when(half == 1)
    def _():
        q_over.start()

    grad_gather = to_group(lambda peer: r.coarse_grad_b, r.gg.at[mine, :])

    def block_of(step):
        j = step // 2
        dy = j + (j // 2) * (5 - 2 * j)
        return lax.rem(y + dy, 4) * 2 + lax.rem(core + step, 2)

    def score(q_all, key_block, piece, slot):
        kk, u = piece
        st = lax.dot_general(
            r.k_all[key_block, kk * WIDE : (kk + 1) * WIDE], q_all[u * WIDE : (u + 1) * WIDE],
            contract_last, preferred_element_type=f32,
        )
        if slot is None:
            return st
        r.scores[slot] = st
        r.tops[slot] = jnp.max(st, axis=0, keepdims=True)

    def absorb(state, st, top, key_block, piece):
        m_all, l_all, acc_all = state
        kk, u = piece
        cols = slice(u * WIDE, (u + 1) * WIDE)
        older = m_all[:, cols]
        fresh = jnp.maximum(older, top)
        weights = jnp.exp2((st - fresh) * POWER)
        factor = jnp.exp2((older - fresh) * POWER)
        m_all[:, cols] = fresh
        l_all[:, cols] = l_all[:, cols] * factor + jnp.sum(weights, axis=0, keepdims=True)
        acc_all[:, cols] = acc_all[:, cols] * factor + jnp.dot(
            r.vt_all[key_block, :, kk * WIDE : (kk + 1) * WIDE], weights.astype(bf16),
            preferred_element_type=f32,
        )

    pieces = [(kk, u) for kk in range(2) for u in range(2)]

    def sweep(q_all, state, first, last, index):
        score(q_all, index(first), pieces[0], 0)

        @pl.loop(first, last)
        def _(step):
            here, then = index(step), index(jnp.minimum(step + 1, last - 1))
            for i, piece in enumerate(pieces):
                if i + 1 < len(pieces):
                    score(q_all, here, pieces[i + 1], (i + 1) % 2)
                else:
                    score(q_all, then, pieces[0], (i + 1) % 2)
                absorb(state, r.scores[i % 2], r.tops[i % 2], here, piece)

    own_state = (r.m_own, r.l_own, r.acc_own)
    far_state = (r.m_far, r.l_far, r.acc_far)

    def arrived(first, last):
        @pl.when(half == 0)
        def _():
            sweep(r.q_far, far_state, first, last, block_of)

        @pl.when(half == 1)
        def _():
            @pl.loop(max(first, 1), last)
            def _(step):
                @pl.when(block_of(step) < block)
                def _():
                    sweep(r.q_own, own_state, step, step + 1, block_of)

    for piece in ((0, 0), (0, 1), (1, 1)):
        st = score(r.q_own, block, piece, None)
        if piece[0] == piece[1]:
            key_pos = lax.broadcasted_iota(jnp.int32, st.shape, 0)
            query_pos = lax.broadcasted_iota(jnp.int32, st.shape, 1)
            st = jnp.where(key_pos <= query_pos, st, very_low)
        absorb(own_state, st, jnp.max(st, axis=0, keepdims=True), block, piece)

    def to_columns(rows_ref, gathered, sem):
        copies = []
        for part in range(2):
            dst = gathered.at[part, aligned(block, group), :]
            for off in range(1, 8):
                peer = lax.rem(block + off, 8)
                copies.append(remote(rows_ref.at[:, lanes(part * 8 + peer)], dst, (half * 8 + peer, t)))
            kept = pltpu.make_async_copy(
                rows_ref.at[:, lanes(part * 8 + block)], dst, r.local.at[sem + part]
            )
            kept.start()
            kept.wait()
        return go(copies)

    landed([k_ring[2], v_ring[2]])

    @pl.when(half == 0)
    def _():
        q_over.wait_recv()

    arrived(0, 2)
    k_below, v_below = r.k_all.at[block_of(4)], r.vt_all.at[block_of(4)]
    k_above, v_above = r.k_all.at[block_of(2)], r.vt_all.at[block_of(2)]
    k_across, v_across = r.k_all.at[block_of(6)], r.vt_all.at[block_of(6)]
    landed(k_ring[:1])
    k_on = go([remote(k_below, k_below, (up, t)), remote(k_below, k_below, (sib, t))])
    landed(v_ring[:1])
    v_on = go([remote(v_above, v_above, (down, t)), remote(v_above, v_above, (sib, t))])
    landed(k_ring[1:2])
    k_on += go([remote(k_above, k_above, (sib, t))])
    landed(v_ring[1:2])
    v_on += go([remote(v_below, v_below, (sib, t))])
    arrived(2, 3)
    landed([k_on[2], v_on[1]])
    arrived(3, 4)
    landed([k_on[1], v_on[2]])
    landed(grad_gather)
    grad_columns = to_columns(r.gg, r.gg_all, 12)
    landed(k_on[:1])
    k_last = go([remote(k_across, k_across, (sib, t))])
    landed(v_on[:1])
    v_last = go([remote(v_across, v_across, (sib, t))])
    arrived(4, 7)
    landed(k_last + v_last)
    arrived(7, 8)

    o_over = remote(r.o_out, r.o_in, (partner, t), always=False)
    stat_over = remote(r.stat_out, r.stat_in, (partner, t), always=False)

    @pl.when(half == 0)
    def _():
        r.o_out[...] = (r.acc_far[...] / r.l_far[...]).astype(bf16)
        r.stat_out[0:1] = r.m_far[...]
        r.stat_out[1:2] = r.l_far[...]
        o_over.start()
        stat_over.start()
        r.o_in[...] = jnp.zeros(r.o_in.shape, bf16)
        r.stat_in[0:1] = jnp.full(r.m_far.shape, very_low, f32)
        r.stat_in[1:2] = jnp.zeros(r.l_far.shape, f32)
        sweep(r.q_own, own_state, 0, block, lambda step: step)

    @pl.when(half == 1)
    def _():
        o_over.wait_recv()
        stat_over.wait_recv()

    other_m, other_l = r.stat_in[0:1], r.stat_in[1:2]
    top = jnp.maximum(r.m_own[...], other_m)
    share = jnp.exp2((r.m_own[...] - top) * POWER)
    other = other_l * jnp.exp2((other_m - top) * POWER)
    total = r.l_own[...] * share + other
    share, other = share / total, other / total
    for h in range(TP):
        cols = slice(h * tok, (h + 1) * tok)
        mixed = r.acc_own[:, cols] * share[:, cols] + r.o_in[:, cols].astype(f32) * other[:, cols]
        r.o_rows[h] = mixed.T.astype(bf16)
    back = to_group(lambda peer: r.o_rows.at[peer], r.att.at[:, lanes(t)])
    own_back = pltpu.make_async_copy(r.o_rows.at[t], r.att.at[:, lanes(t)], r.local.at[14])
    own_back.start()
    own_back.wait()
    loads["out_w"].wait()
    loads["fine"].wait()
    landed(back)

    projected = jnp.dot(r.att[...], r.out_w[...], preferred_element_type=f32)
    r.stream[...] = (r.fine[...].astype(f32) + projected).astype(bf16)
    border_copy = remote(r.stream.at[pl.ds(tok - 16, 16), :], r.border, after)
    border_copy.start()
    window = jnp.where((col >= row * SHORTEN - (SHORTEN - 1)) & (col <= row * SHORTEN), 1.0, 0.0)
    coarse = jnp.dot(window.astype(bf16), r.stream[...], preferred_element_type=f32)
    edge_row = lax.broadcasted_iota(jnp.int32, (crows, 16), 0)
    edge_col = lax.broadcasted_iota(jnp.int32, (crows, 16), 1)
    edge = jnp.where((edge_row == 0) & (edge_col > 16 - SHORTEN) & (flat > 0), 1.0, 0.0)
    border_copy.wait_recv()
    coarse = coarse + jnp.dot(edge.astype(bf16), r.border[...], preferred_element_type=f32)
    coarse = coarse / SHORTEN
    rstd = lax.rsqrt(jnp.mean(coarse * coarse, axis=-1, keepdims=True) + 1e-05)
    base = coarse * rstd
    r.coarse_b[...] = (base * gain_ref[...]).astype(bf16)
    r.ng[mine, :] = r.coarse_b[...]
    norm_gather = to_group(lambda peer: r.coarse_b, r.ng.at[mine, :])

    loads["down_w"].wait()
    r.hidden_grad[...] = lax.dot_general(
        r.gg[...], r.down_w[...], contract_last, preferred_element_type=f32
    )
    loads["gate_w"].wait()
    loads["up_w"].wait()

    landed(norm_gather)
    gate = lax.dot_general(r.ng[...], r.gate_w[...], contract_last, preferred_element_type=f32)
    up_v = lax.dot_general(r.ng[...], r.up_w[...], contract_last, preferred_element_type=f32)
    sig = jax.nn.sigmoid(gate)
    act = gate * sig
    above, below, across = (lax.rem(y + dy, 4) * 2 + core for dy in (1, 3, 2))
    cut = group // 2
    parts = (pl.ds(0, cut), pl.ds(cut, cut), pl.ds(0, group))

    def ring(i, source, piece, device):
        ref = r.hgu.at[i, source, parts[piece], :]
        return remote(ref, ref, (device, t))

    def around(i):
        return (
            go([ring(i, block, 0, up), ring(i, block, 1, up)]),
            go([ring(i, block, 1, down), ring(i, block, 0, down)]),
            go([ring(i, block, 2, sib)]),
        )

    rings = []
    r.hgu[0, block] = (act * up_v).astype(bf16)
    rings.append(around(0))
    r.hgu[1, block] = (
        r.hidden_grad[...] * up_v * sig * (1.0 + gate * (1.0 - sig))
    ).astype(bf16)
    rings.append(around(1))
    r.hgu[2, block] = (r.hidden_grad[...] * act).astype(bf16)
    rings.append(around(2))

    part = jnp.dot(r.hgu[0, block], r.down_w[...], preferred_element_type=f32)
    r.down_out[...] = part.astype(bf16).reshape(r.down_out.shape)
    r.down_in[t] = r.down_out[t]
    down_sum = to_group(lambda peer: r.down_out.at[peer], r.down_in.at[t])
    part = jnp.dot(r.hgu[1, block], r.gate_w[...], preferred_element_type=f32) + jnp.dot(
        r.hgu[2, block], r.up_w[...], preferred_element_type=f32
    )
    r.norm_out[...] = part.astype(bf16).reshape(r.norm_out.shape)
    r.norm_in[t] = r.norm_out[t]
    norm_sum = to_group(lambda peer: r.norm_out.at[peer], r.norm_in.at[t])
    norm_columns = to_columns(r.ng, r.ng_all, 15)

    def pass_on(i):
        ring_up, ring_down, _ = rings[i]
        landed(ring_up[:1])
        first = go([ring(i, below, 0, up)])
        landed(ring_down[:1])
        first += go([ring(i, above, 1, down)])
        landed(ring_up[1:])
        rest = go([ring(i, below, 2, sib)])
        landed(ring_down[1:])
        rest += go([ring(i, above, 2, sib)])
        return first, rest

    def pass_last(i):
        landed(on[i][0])
        return go([ring(i, across, 2, sib)])

    on, last = [pass_on(0)], []

    landed(down_sum)
    coarse_out = coarse + jnp.sum(r.down_in[...].astype(f32), axis=0)
    spread = (crows, SHORTEN, D)
    section_ref[...] = (
        (r.stream[...].astype(f32).reshape(spread) + coarse_out[:, None, :])
        .reshape(tok, D)
        .astype(bf16)
    )
    on.append(pass_on(1))
    last.append(pass_last(0))

    landed(norm_sum)
    normed_grad = jnp.sum(r.norm_in[...].astype(f32), axis=0)
    width = D // 8

    def fold_row(ref, value):
        for i in range(8):
            ref[i : i + 1, :] = value[:, i * width : (i + 1) * width]

    def flat_row(ref):
        return jnp.concatenate([ref[i : i + 1, :] for i in range(8)], axis=1)

    scaled = normed_grad * gain_ref[...]
    coarse_total = r.coarse_grad[...] + rstd * (
        scaled - base * jnp.mean(scaled * base, axis=-1, keepdims=True)
    )
    fold_row(r.follow_out, coarse_total[0:1])
    follow = remote(r.follow_out, r.follow_in, before)
    follow.start()
    fold_row(r.gain_out, jnp.sum(normed_grad * base, axis=0, keepdims=True))
    r.gain_in[t] = r.gain_out[...]
    gain_sum = to_group(lambda peer: r.gain_out, r.gain_in.at[t])

    on.append(pass_on(2))
    last.append(pass_last(1))

    follow.wait_recv()
    following = jnp.where(flat < number - 1, flat_row(r.follow_in), 0.0)
    ahead = jnp.concatenate([coarse_total[1:], following], axis=0)
    place = lax.broadcasted_iota(jnp.int32, spread, 1)
    contrib = jnp.where(place == 0, coarse_total[:, None, :], ahead[:, None, :])
    stream_grad_ref[...] = (
        (r.cot[...].astype(f32).reshape(spread) + contrib / SHORTEN).reshape(tok, D).astype(bf16)
    )
    last.append(pass_last(2))

    landed(gain_sum)
    r.gain_mid[...] = jnp.sum(r.gain_in[...], axis=0)
    r.gain_half[block] = r.gain_mid[...]
    gain_group = go([
        remote(r.gain_mid, r.gain_half.at[block], (half * 8 + lax.rem(block + off, 8), t))
        for off in range(1, 8)
    ])

    landed(grad_columns + norm_columns)
    outs = (down_grad_ref, gate_grad_ref, up_grad_ref)

    def term(i, part):
        right = (r.gg_all if i == 0 else r.ng_all)[part]
        left = r.hgu[i].reshape(8 * group, hid)
        return lax.dot_general(left, right, contract_first, preferred_element_type=f32)

    terms = []
    for i in range(3):
        landed(rings[i][2] + on[i][1] + last[i])
        r.term_out[i] = term(i, 1 - half).astype(bf16)
        terms += go([remote(r.term_out.at[i], r.term_in.at[i], (partner, t))])
    landed(gain_group)
    r.gain_far_out[...] = jnp.sum(r.gain_half[...], axis=0)
    gain_far = remote(r.gain_far_out, r.gain_far_in, (partner, t))
    gain_far.start()
    for i in range(3):
        outs[i][...] = term(i, half)
    gain_far.wait_recv()
    gain_grad_ref[...] = flat_row(r.gain_far_out) + flat_row(r.gain_far_in)
    for i in range(3):
        terms[i].wait_recv()
        outs[i][...] = outs[i][...] + r.term_in[i].astype(f32)

    for cp in used:
        cp.wait_send()

    @pl.when(half == 1)
    def _():
        q_over.wait_send()

    @pl.when(half == 0)
    def _():
        o_over.wait_send()
        stat_over.wait_send()


def hand_over_kernel(*refs):
    count = len(refs) // 2
    copies = [
        pltpu.make_async_copy(src, dst, refs[-1].at[i])
        for i, (src, dst) in enumerate(zip(refs[:count], refs[count:-1]))
    ]
    for cp in copies:
        cp.start()
    for cp in copies:
        cp.wait()


def on_device(
    fine_stream,
    queries,
    keys,
    values,
    out_weight,
    norm_gain,
    gate_weight,
    up_weight,
    down_weight,
    cotangent,
):
    tok = fine_stream.shape[0]
    hid = gate_weight.shape[1]
    seq = lax.axis_size("seq")
    f32, bf16 = jnp.float32, jnp.bfloat16
    vmem, anywhere = pl.BlockSpec(memory_space=pltpu.VMEM), pl.BlockSpec(memory_space=pl.ANY)
    scratch = scratch_of(tok, hid, seq)
    shapes = (
        jax.ShapeDtypeStruct((tok, D), bf16),
        jax.ShapeDtypeStruct((tok, D), bf16),
        jax.ShapeDtypeStruct((hid, D // seq), f32),
        jax.ShapeDtypeStruct((hid, D // seq), f32),
        jax.ShapeDtypeStruct((hid, D // seq), f32),
        jax.ShapeDtypeStruct((1, D), f32),
    )
    outs = pl.pallas_call(
        lambda *refs: section_kernel(tuple(scratch), *refs),
        out_shape=shapes,
        in_specs=[anywhere] * 5 + [vmem] + [anywhere] * 4,
        out_specs=(vmem,) * 6,
        scratch_shapes=list(scratch.values()),
        compiler_params=pltpu.CompilerParams(
            collective_id=0, has_side_effects=True, vmem_limit_bytes=60 * 1024 * 1024
        ),
        name="section",
    )(
        queries, keys, values, fine_stream, cotangent, norm_gain.reshape(1, D),
        out_weight, gate_weight.T, up_weight.T, down_weight,
    )
    section_out, stream_grad, gate_grad, up_grad, down_grad, gain_grad = pl.pallas_call(
        hand_over_kernel,
        out_shape=shapes,
        in_specs=[anywhere] * 6,
        out_specs=(anywhere,) * 6,
        scratch_shapes=[pltpu.SemaphoreType.DMA((6,))],
        name="hand_over",
    )(*outs)
    return (section_out, stream_grad, gate_grad.T, up_grad.T, down_grad, gain_grad.reshape(D))


def solution(mesh):
    return jax.shard_map(
        on_device,
        mesh=mesh,
        in_specs=(
            P(("seq", "tp"), None),
            P(("seq", "tp"), None),
            P(("seq", "tp"), None),
            P(("seq", "tp"), None),
            P(),
            P(),
            P(None, "tp"),
            P(None, "tp"),
            P("tp", None),
            P(("seq", "tp"), None),
        ),
        out_specs=(
            P(("seq", "tp"), None),
            P(("seq", "tp"), None),
            P("seq", "tp"),
            P("seq", "tp"),
            P("tp", "seq"),
            P(),
        ),
        check_vma=False,
    )
```

time: 627 us -> 184 us (0.29)
  waiting for transfers between devices: 377 us -> 0 us
  Pallas kernels: 0 us -> 180 us
  blocking collectives: 152 us -> 0 us
  local copies, waits for them, and re-layouts: 27 us -> 0 us
  matrix products: 26.4 us -> 0 us
  other arithmetic: 14.7 us -> 0 us
  between operations: 14.4 us -> 0.8 us
  starting transfers between devices: 12.5 us -> 0 us
    pallas_call x0 -> x2, Pallas kernels: none -> 180 us  [the longest x1 115 us: on_device(): pl.pallas_call(lambda *refs: section_kernel(tuple(scratch), *refs), out_s...]
    unnamed x10 -> x0, waiting for transfers between devices: 157 us -> none
    reduce_scatter x2 -> x0, waiting for transfers between devices: 128 us -> none  [the longest x1 89.8 us: on_device(): lax.psum_scatter((lax.dot_general(gate_delta, gate_weight, contract_last,...]
    all_gather x2 -> x0, waiting for transfers between devices: 85.3 us -> none  [the longest x1 55.5 us: on_device(): value_piece = lax.all_gather(v_heads, 'seq', axis=0, tiled=True)]
    psum x1 -> x0, blocking collectives: 66.9 us -> none  [on_device(): gain_grad = lax.psum(jnp.sum(normed_grad * base, axis=0), ('seq', 'tp'))]
    all_gather x2 -> x0, blocking collectives: 61.6 us -> none  [the longest x1 31.2 us: on_device(): grad_group = lax.all_gather(coarse_grad_b, 'tp', axis=0, tiled=True)]
    dot_general x12 -> x0, matrix products: 26.4 us -> none  [the longest x1 3.42 us: on_device(): lax.dot_general(normed_group, up_delta, contract_first, preferred_element...]
    all_to_all x2 -> x0, blocking collectives: 23.9 us -> none  [the longest x1 13.5 us: on_device(): lax.all_to_all(keys, 'tp', split_axis=1, concat_axis=0, tiled=True)]
  transfers between devices with their start and end apart: 11 -> 0, of which waited for: 9 -> 0; matrix products, arithmetic and copies ran while one was open for 7% -> 0% of each run, Pallas kernels for 0% -> 0%
where the time goes in v3:
time: 184 us; the launch traced here: 181 us
  Pallas kernels  180 us (98%)
    pallas_call x1, Pallas kernels, on_device(): pl.pallas_call(lambda *refs: section_kernel(tuple(scratch), *refs), out_s...  115 us
    pallas_call x1, Pallas kernels, on_device(): pl.pallas_call(hand_over_kernel, out_shape=shapes, in_specs=[anywhere] *...  65.9 us

profile of v3, /device:TPU:0, one launch (start us, length us, event | category | flops | bytes accessed | tf_op | source)
XLA Modules:
  0.0 181.3 jit_solution(9207212724898685204)
XLA Ops:
  0.6 114.6 %section.1 = (bf16[128,2048]{1,0:T(8,128)(2,1)}, bf16[128,2048]{1,0:T(8,128)(2,1)}, f32[704,128]{1,0:T(8,128)}, f32[704,128]{1,0:T(8,128)}, f32[704,128]{1,0:T(8,128)}, /*index=5*/f32[1,2048]{1,0:T(1,128)}) custom-call(bf16[128,1024]{1,0:T(8,128)(2,1)} %refs_0_.1, bf16[128,1024]{1,0:T(8,128)(2,1)} %refs_1_.1, bf16[128,1024]{1,0:T(8,128)(2,1)} %refs_2_.1, ...), custom_call_target="tpu_custom_call" | custom-call | tf_op jit(solution)/shard_map/section/pallas_call | solution.py:576
  115.2 65.9 %hand_over.1 = (bf16[128,2048]{1,0:T(8,128)(2,1)}, bf16[128,2048]{1,0:T(8,128)(2,1)}, f32[704,128]{1,0:T(8,128)}, f32[704,128]{1,0:T(8,128)}, f32[704,128]{1,0:T(8,128)}, /*index=5*/f32[1,2048]{1,0:T(1,128)}) custom-call(bf16[128,2048]{1,0:T(8,128)(2,1)} %get-tuple-element.18.refs_0_, bf16[128,2048]{1,0:T(8,128)(2,1)} %get-tuple-element.19.refs_1_, ...), custom_call_target="tpu_custom_call" | custom-call | tf_op jit(solution)/shard_map/hand_over/pallas_call | solution.py:590

commit v4 on v3

--- a/solution.py
+++ b/solution.py
@@ -115,12 +115,14 @@
     hid = r.gate_w.shape[0]
 
     loads = {}
-    for name, src in (
-        ("k_in", k_hbm), ("v_in", v_hbm), ("q_in", q_hbm), ("cot", cot_hbm), ("fine", fine_hbm),
-        ("out_w", out_hbm), ("down_w", down_hbm), ("gate_w", gate_hbm), ("up_w", up_hbm),
-    ):
+
+    def load(name, src):
         loads[name] = pltpu.make_async_copy(src, getattr(r, name), r.local.at[len(loads)])
         loads[name].start()
+
+    load("k_in", k_hbm)
+    load("v_in", v_hbm)
+    load("q_in", q_hbm)
 
     barrier = pltpu.get_barrier_semaphore()
     peers = [(s, lax.rem(t + off, TP)) for off in range(1, TP)]
@@ -179,6 +181,8 @@
         pltpu.make_async_copy(r.vt_src.at[t], r.vt_all.at[block, :, band], r.local.at[11]),
     ])
 
+    load("cot", cot_hbm)
+
     mine = aligned(t, crows)
     row = lax.broadcasted_iota(jnp.int32, (crows, tok), 0)
     col = lax.broadcasted_iota(jnp.int32, (crows, tok), 1)
@@ -203,6 +207,11 @@
         q_over.start()
 
     grad_gather = to_group(lambda peer: r.coarse_grad_b, r.gg.at[mine, :])
+    load("out_w", out_hbm)
+    load("fine", fine_hbm)
+    load("down_w", down_hbm)
+    load("gate_w", gate_hbm)
+    load("up_w", up_hbm)
 
     def block_of(step):
         j = step // 2
@@ -310,8 +319,6 @@
     landed([k_on[2], v_on[1]])
     arrived(3, 4)
     landed([k_on[1], v_on[2]])
-    landed(grad_gather)
-    grad_columns = to_columns(r.gg, r.gg_all, 12)
     landed(k_on[:1])
     k_last = go([remote(k_across, k_across, (sib, t))])
     landed(v_on[:1])
@@ -333,6 +340,12 @@
         r.o_in[...] = jnp.zeros(r.o_in.shape, bf16)
         r.stat_in[0:1] = jnp.full(r.m_far.shape, very_low, f32)
         r.stat_in[1:2] = jnp.zeros(r.l_far.shape, f32)
+
+    landed(grad_gather)
+    grad_columns = to_columns(r.gg, r.gg_all, 12)
+
+    @pl.when(half == 0)
+    def _():
         sweep(r.q_own, own_state, 0, block, lambda step: step)
 
     @pl.when(half == 1)
@@ -384,6 +397,7 @@
     loads["up_w"].wait()
 
     landed(norm_gather)
+    norm_columns = to_columns(r.ng, r.ng_all, 15)
     gate = lax.dot_general(r.ng[...], r.gate_w[...], contract_last, preferred_element_type=f32)
     up_v = lax.dot_general(r.ng[...], r.up_w[...], contract_last, preferred_element_type=f32)
     sig = jax.nn.sigmoid(gate)
@@ -423,7 +437,6 @@
     r.norm_out[...] = part.astype(bf16).reshape(r.norm_out.shape)
     r.norm_in[t] = r.norm_out[t]
     norm_sum = to_group(lambda peer: r.norm_out.at[peer], r.norm_in.at[t])
-    norm_columns = to_columns(r.ng, r.ng_all, 15)
 
     def pass_on(i):
         ring_up, ring_down, _ = rings[i]
@@ -536,14 +549,17 @@
 
 
 def hand_over_kernel(*refs):
-    count = len(refs) // 2
-    copies = [
-        pltpu.make_async_copy(src, dst, refs[-1].at[i])
-        for i, (src, dst) in enumerate(zip(refs[:count], refs[count:-1]))
-    ]
-    for cp in copies:
+    count = (len(refs) - 2) // 3
+    ins, outs, held = refs[:count], refs[count : 2 * count], refs[2 * count : 3 * count]
+    arrive, leave = refs[-2:]
+    first = [pltpu.make_async_copy(a, b, arrive.at[i]) for i, (a, b) in enumerate(zip(ins, held))]
+    second = [pltpu.make_async_copy(a, b, leave.at[i]) for i, (a, b) in enumerate(zip(held, outs))]
+    for cp in first:
         cp.start()
-    for cp in copies:
+    for one, two in zip(first, second):
+        one.wait()
+        two.start()
+    for cp in second:
         cp.wait()
 
 
@@ -563,7 +579,7 @@
     hid = gate_weight.shape[1]
     seq = lax.axis_size("seq")
     f32, bf16 = jnp.float32, jnp.bfloat16
-    vmem, anywhere = pl.BlockSpec(memory_space=pltpu.VMEM), pl.BlockSpec(memory_space=pl.ANY)
+    vmem, hbm = pl.BlockSpec(memory_space=pltpu.VMEM), pl.BlockSpec(memory_space=pltpu.HBM)
     scratch = scratch_of(tok, hid, seq)
     shapes = (
         jax.ShapeDtypeStruct((tok, D), bf16),
@@ -576,7 +592,7 @@
     outs = pl.pallas_call(
         lambda *refs: section_kernel(tuple(scratch), *refs),
         out_shape=shapes,
-        in_specs=[anywhere] * 5 + [vmem] + [anywhere] * 4,
+        in_specs=[hbm] * 5 + [vmem] + [hbm] * 4,
         out_specs=(vmem,) * 6,
         scratch_shapes=list(scratch.values()),
         compiler_params=pltpu.CompilerParams(
@@ -590,9 +606,11 @@
     section_out, stream_grad, gate_grad, up_grad, down_grad, gain_grad = pl.pallas_call(
         hand_over_kernel,
         out_shape=shapes,
-        in_specs=[anywhere] * 6,
-        out_specs=(anywhere,) * 6,
-        scratch_shapes=[pltpu.SemaphoreType.DMA((6,))],
+        in_specs=[hbm] * 6,
+        out_specs=(hbm,) * 6,
+        scratch_shapes=[pltpu.VMEM(shape.shape, shape.dtype) for shape in shapes]
+        + [pltpu.SemaphoreType.DMA((6,)), pltpu.SemaphoreType.DMA((6,))],
+        compiler_params=pltpu.CompilerParams(vmem_limit_bytes=60 * 1024 * 1024),
         name="hand_over",
     )(*outs)
     return (section_out, stream_grad, gate_grad.T, up_grad.T, down_grad, gain_grad.reshape(D))

time: 184 us -> 118 us (0.64)
  the two profiles are of different devices: /device:TPU:0 before, /device:TPU:8 now
where the time goes in v4:
time: 118 us
  Pallas kernels  117 us (99%)
    pallas_call x1, Pallas kernels, on_device(): pl.pallas_call(lambda *refs: section_kernel(tuple(scratch), *refs), out_s...  115 us
    pallas_call x1, Pallas kernels, on_device(): pl.pallas_call(hand_over_kernel, out_shape=shapes, in_specs=[hbm] * 6, ou...  2.47 us

profile of v4, /device:TPU:8, one launch (start us, length us, event | category | flops | bytes accessed | tf_op | source)
XLA Modules:
  0.0 118.0 jit_solution(165670854592812965)
XLA Ops:
  0.6 114.8 %section.1 = (bf16[128,2048]{1,0:T(8,128)(2,1)}, bf16[128,2048]{1,0:T(8,128)(2,1)}, f32[704,128]{1,0:T(8,128)}, f32[704,128]{1,0:T(8,128)}, f32[704,128]{1,0:T(8,128)}, /*index=5*/f32[1,2048]{1,0:T(1,128)}) custom-call(bf16[128,1024]{1,0:T(8,128)(2,1)} %refs_0_.1, bf16[128,1024]{1,0:T(8,128)(2,1)} %refs_1_.1, bf16[128,1024]{1,0:T(8,128)(2,1)} %refs_2_.1, ...), custom_call_target="tpu_custom_call" | custom-call | tf_op jit(solution)/shard_map/section/pallas_call | solution.py:592
  115.4 2.5 %hand_over.1 = (bf16[128,2048]{1,0:T(8,128)(2,1)}, bf16[128,2048]{1,0:T(8,128)(2,1)}, f32[704,128]{1,0:T(8,128)}, f32[704,128]{1,0:T(8,128)}, f32[704,128]{1,0:T(8,128)}, /*index=5*/f32[1,2048]{1,0:T(1,128)}) custom-call(bf16[128,2048]{1,0:T(8,128)(2,1)} %get-tuple-element.18.refs_0_, bf16[128,2048]{1,0:T(8,128)(2,1)} %get-tuple-element.19.refs_1_, ...), custom_call_target="tpu_custom_call" | custom-call | tf_op jit(solution)/shard_map/hand_over/pallas_call | solution.py:606

commit v5 on v4

--- a/solution.py
+++ b/solution.py
@@ -13,7 +13,7 @@
 MESH = pl.DeviceIdType.MESH
 TP = 8
 WIDE = 512
-COPIES = 160
+COPIES = 190
 
 contract_last = (((1,), (1,)), ((), ()))
 contract_first = (((0,), (0,)), ((), ()))
@@ -49,22 +49,26 @@
         "m_far": vmem((1, rows), f32),
         "l_far": vmem((1, rows), f32),
         "acc_far": vmem((HEAD, rows), f32),
-        "o_out": vmem((HEAD, rows), bf16),
-        "o_in": vmem((HEAD, rows), bf16),
-        "stat_out": vmem((8, rows), f32),
-        "stat_in": vmem((8, rows), f32),
-        "o_rows": vmem((TP, tok, HEAD), bf16),
-        "att": vmem((tok, TP * HEAD), bf16),
+        "o_own": vmem((HEAD, rows), bf16),
+        "o_far": vmem((HEAD, rows), bf16),
+        "stat_own": vmem((8, rows), f32),
+        "stat_far": vmem((8, rows), f32),
+        "own_in": vmem((TP, HEAD, tok), bf16),
+        "far_in": vmem((TP, HEAD, tok), bf16),
+        "own_stat_in": vmem((TP, 8, tok), f32),
+        "far_stat_in": vmem((TP, 8, tok), f32),
+        "att": vmem((TP * HEAD, tok), bf16),
         "stream": vmem((tok, D), bf16),
-        "border": vmem((16, D), bf16),
+        "border_out": vmem(small, f32),
+        "border_in": vmem(small, f32),
         "coarse_b": vmem((crows, D), bf16),
         "coarse_grad": vmem((crows, D), f32),
         "coarse_grad_b": vmem((crows, D), bf16),
         "ng": vmem((group, D), bf16),
         "gg": vmem((group, D), bf16),
         "hidden_grad": vmem((group, hid), f32),
-        "ng_all": vmem((2, 8 * group, HEAD), bf16),
-        "gg_all": vmem((2, 8 * group, HEAD), bf16),
+        "ng_all": vmem((8 * group, 2 * HEAD), bf16),
+        "gg_all": vmem((8 * group, 2 * HEAD), bf16),
         "hgu": vmem((3, 8, group, hid), bf16),
         "down_out": vmem((TP, crows, D), bf16),
         "down_in": vmem((TP, crows, D), bf16),
@@ -78,6 +82,7 @@
         "gain_half": vmem((8,) + small, f32),
         "gain_far_out": vmem(small, f32),
         "gain_far_in": vmem(small, f32),
+        "term": vmem((3, hid, 2 * HEAD), f32),
         "term_out": vmem((3, hid, HEAD), bf16),
         "term_in": vmem((3, hid, HEAD), bf16),
         "send": pltpu.SemaphoreType.DMA((COPIES,)),
@@ -127,7 +132,7 @@
     barrier = pltpu.get_barrier_semaphore()
     peers = [(s, lax.rem(t + off, TP)) for off in range(1, TP)]
     peers += [(half * 8 + lax.rem(block + off, 8), t) for off in range(1, 8)]
-    peers += [(partner, t), after, before]
+    peers += [(partner, lax.rem(t + off, TP)) for off in range(TP)] + [after, before]
     for peer in peers:
         pl.semaphore_signal(barrier, inc=1, device_id=peer, device_id_type=MESH)
     for ref, value in ((r.m_own, very_low), (r.l_own, 0.0), (r.acc_own, 0.0),
@@ -170,6 +175,15 @@
 
     def lanes(index):
         return aligned(index, HEAD)
+
+    width = D // 8
+
+    def fold_row(ref, value):
+        for i in range(8):
+            ref[i : i + 1, :] = value[:, i * width : (i + 1) * width]
+
+    def flat_row(ref):
+        return jnp.concatenate([ref[i : i + 1, :] for i in range(8)], axis=1)
 
     band = aligned(t, tok)
     k_copies = to_group(lambda peer: r.k_in.at[:, lanes(peer)], r.k_all.at[block, band, :])
@@ -286,7 +300,7 @@
     def to_columns(rows_ref, gathered, sem):
         copies = []
         for part in range(2):
-            dst = gathered.at[part, aligned(block, group), :]
+            dst = gathered.at[aligned(block, group), part * HEAD : (part + 1) * HEAD]
             for off in range(1, 8):
                 peer = lax.rem(block + off, 8)
                 copies.append(remote(rows_ref.at[:, lanes(part * 8 + peer)], dst, (half * 8 + peer, t)))
@@ -327,61 +341,71 @@
     landed(k_last + v_last)
     arrived(7, 8)
 
-    o_over = remote(r.o_out, r.o_in, (partner, t), always=False)
-    stat_over = remote(r.stat_out, r.stat_in, (partner, t), always=False)
+    def normalized(state, out, stat):
+        m_all, l_all, acc_all = state
+        out[...] = (acc_all[...] / l_all[...]).astype(bf16)
+        stat[0:1] = m_all[...]
+        stat[1:2] = l_all[...]
+
+    far_back = []
+    for off in range(TP):
+        peer = lax.rem(t + off, TP)
+        far_back += [
+            remote(r.o_far.at[:, lanes(peer)], r.far_in.at[t], (partner, peer), always=False),
+            remote(r.stat_far.at[:, lanes(peer)], r.far_stat_in.at[t], (partner, peer), always=False),
+        ]
 
     @pl.when(half == 0)
     def _():
-        r.o_out[...] = (r.acc_far[...] / r.l_far[...]).astype(bf16)
-        r.stat_out[0:1] = r.m_far[...]
-        r.stat_out[1:2] = r.l_far[...]
-        o_over.start()
-        stat_over.start()
-        r.o_in[...] = jnp.zeros(r.o_in.shape, bf16)
-        r.stat_in[0:1] = jnp.full(r.m_far.shape, very_low, f32)
-        r.stat_in[1:2] = jnp.zeros(r.l_far.shape, f32)
-
+        normalized(far_state, r.o_far, r.stat_far)
+        go(far_back)
+        r.far_in[...] = jnp.zeros(r.far_in.shape, bf16)
+        r.far_stat_in[:, 0:1] = jnp.full((TP, 1, tok), very_low, f32)
+        r.far_stat_in[:, 1:2] = jnp.zeros((TP, 1, tok), f32)
+        sweep(r.q_own, own_state, 0, block, lambda step: step)
+
+    normalized(own_state, r.o_own, r.stat_own)
+    back = to_group(lambda peer: r.o_own.at[:, lanes(peer)], r.own_in.at[t])
+    back += to_group(lambda peer: r.stat_own.at[:, lanes(peer)], r.own_stat_in.at[t])
+    kept = go([
+        pltpu.make_async_copy(r.o_own.at[:, lanes(t)], r.own_in.at[t], r.local.at[14]),
+        pltpu.make_async_copy(r.stat_own.at[:, lanes(t)], r.own_stat_in.at[t], r.local.at[17]),
+    ])
     landed(grad_gather)
     grad_columns = to_columns(r.gg, r.gg_all, 12)
-
-    @pl.when(half == 0)
-    def _():
-        sweep(r.q_own, own_state, 0, block, lambda step: step)
-
-    @pl.when(half == 1)
-    def _():
-        o_over.wait_recv()
-        stat_over.wait_recv()
-
-    other_m, other_l = r.stat_in[0:1], r.stat_in[1:2]
-    top = jnp.maximum(r.m_own[...], other_m)
-    share = jnp.exp2((r.m_own[...] - top) * POWER)
-    other = other_l * jnp.exp2((other_m - top) * POWER)
-    total = r.l_own[...] * share + other
-    share, other = share / total, other / total
-    for h in range(TP):
-        cols = slice(h * tok, (h + 1) * tok)
-        mixed = r.acc_own[:, cols] * share[:, cols] + r.o_in[:, cols].astype(f32) * other[:, cols]
-        r.o_rows[h] = mixed.T.astype(bf16)
-    back = to_group(lambda peer: r.o_rows.at[peer], r.att.at[:, lanes(t)])
-    own_back = pltpu.make_async_copy(r.o_rows.at[t], r.att.at[:, lanes(t)], r.local.at[14])
-    own_back.start()
-    own_back.wait()
+    for cp in kept:
+        cp.wait()
     loads["out_w"].wait()
     loads["fine"].wait()
     landed(back)
 
-    projected = jnp.dot(r.att[...], r.out_w[...], preferred_element_type=f32)
+    @pl.when(half == 1)
+    def _():
+        landed(far_back)
+
+    for h in range(TP):
+        own_m, own_l = r.own_stat_in[h, 0:1], r.own_stat_in[h, 1:2]
+        far_m, far_l = r.far_stat_in[h, 0:1], r.far_stat_in[h, 1:2]
+        top = jnp.maximum(own_m, far_m)
+        own_l = own_l * jnp.exp2((own_m - top) * POWER)
+        far_l = far_l * jnp.exp2((far_m - top) * POWER)
+        total = own_l + far_l
+        r.att[h * HEAD : (h + 1) * HEAD] = (
+            r.own_in[h].astype(f32) * (own_l / total) + r.far_in[h].astype(f32) * (far_l / total)
+        ).astype(bf16)
+    projected = lax.dot_general(r.att[...], r.out_w[...], contract_first, preferred_element_type=f32)
     r.stream[...] = (r.fine[...].astype(f32) + projected).astype(bf16)
-    border_copy = remote(r.stream.at[pl.ds(tok - 16, 16), :], r.border, after)
-    border_copy.start()
+    row = lax.broadcasted_iota(jnp.int32, (crows + 8, tok), 0)
+    col = lax.broadcasted_iota(jnp.int32, (crows + 8, tok), 1)
     window = jnp.where((col >= row * SHORTEN - (SHORTEN - 1)) & (col <= row * SHORTEN), 1.0, 0.0)
     coarse = jnp.dot(window.astype(bf16), r.stream[...], preferred_element_type=f32)
-    edge_row = lax.broadcasted_iota(jnp.int32, (crows, 16), 0)
-    edge_col = lax.broadcasted_iota(jnp.int32, (crows, 16), 1)
-    edge = jnp.where((edge_row == 0) & (edge_col > 16 - SHORTEN) & (flat > 0), 1.0, 0.0)
+    fold_row(r.border_out, coarse[crows : crows + 1])
+    border_copy = remote(r.border_out, r.border_in, after)
+    border_copy.start()
     border_copy.wait_recv()
-    coarse = coarse + jnp.dot(edge.astype(bf16), r.border[...], preferred_element_type=f32)
+    edge = jnp.where(flat > 0, flat_row(r.border_in), 0.0)
+    first = lax.broadcasted_iota(jnp.int32, (crows, D), 0) == 0
+    coarse = coarse[:crows] + jnp.where(first, edge, 0.0)
     coarse = coarse / SHORTEN
     rstd = lax.rsqrt(jnp.mean(coarse * coarse, axis=-1, keepdims=True) + 1e-05)
     base = coarse * rstd
@@ -469,15 +493,6 @@
 
     landed(norm_sum)
     normed_grad = jnp.sum(r.norm_in[...].astype(f32), axis=0)
-    width = D // 8
-
-    def fold_row(ref, value):
-        for i in range(8):
-            ref[i : i + 1, :] = value[:, i * width : (i + 1) * width]
-
-    def flat_row(ref):
-        return jnp.concatenate([ref[i : i + 1, :] for i in range(8)], axis=1)
-
     scaled = normed_grad * gain_ref[...]
     coarse_total = r.coarse_grad[...] + rstd * (
         scaled - base * jnp.mean(scaled * base, axis=-1, keepdims=True)
@@ -491,6 +506,30 @@
 
     on.append(pass_on(2))
     last.append(pass_last(1))
+
+    outs = (down_grad_ref, gate_grad_ref, up_grad_ref)
+
+    def term(i):
+        landed(rings[i][2] + on[i][1] + last[i])
+        right = r.gg_all if i == 0 else r.ng_all
+        left = r.hgu[i].reshape(8 * group, hid)
+        r.term[i] = lax.dot_general(left, right[...], contract_first, preferred_element_type=f32)
+        r.term_out[i] = r.term[i, :, lanes(1 - half)].astype(bf16)
+        return go([remote(r.term_out.at[i], r.term_in.at[i], (partner, t))])
+
+    landed(grad_columns)
+    terms = term(0)
+    last.append(pass_last(2))
+
+    landed(gain_sum)
+    r.gain_mid[...] = jnp.sum(r.gain_in[...], axis=0)
+    r.gain_half[block] = r.gain_mid[...]
+    gain_group = go([
+        remote(r.gain_mid, r.gain_half.at[block], (half * 8 + lax.rem(block + off, 8), t))
+        for off in range(1, 8)
+    ])
+    landed(norm_columns)
+    terms += term(1)
 
     follow.wait_recv()
     following = jnp.where(flat < number - 1, flat_row(r.follow_in), 0.0)
@@ -500,35 +539,14 @@
     stream_grad_ref[...] = (
         (r.cot[...].astype(f32).reshape(spread) + contrib / SHORTEN).reshape(tok, D).astype(bf16)
     )
-    last.append(pass_last(2))
-
-    landed(gain_sum)
-    r.gain_mid[...] = jnp.sum(r.gain_in[...], axis=0)
-    r.gain_half[block] = r.gain_mid[...]
-    gain_group = go([
-        remote(r.gain_mid, r.gain_half.at[block], (half * 8 + lax.rem(block + off, 8), t))
-        for off in range(1, 8)
-    ])
-
-    landed(grad_columns + norm_columns)
-    outs = (down_grad_ref, gate_grad_ref, up_grad_ref)
-
-    def term(i, part):
-        right = (r.gg_all if i == 0 else r.ng_all)[part]
-        left = r.hgu[i].reshape(8 * group, hid)
-        return lax.dot_general(left, right, contract_first, preferred_element_type=f32)
-
-    terms = []
-    for i in range(3):
-        landed(rings[i][2] + on[i][1] + last[i])
-        r.term_out[i] = term(i, 1 - half).astype(bf16)
-        terms += go([remote(r.term_out.at[i], r.term_in.at[i], (partner, t))])
+
+    terms += term(2)
     landed(gain_group)
     r.gain_far_out[...] = jnp.sum(r.gain_half[...], axis=0)
     gain_far = remote(r.gain_far_out, r.gain_far_in, (partner, t))
     gain_far.start()
     for i in range(3):
-        outs[i][...] = term(i, half)
+        outs[i][...] = r.term[i, :, lanes(half)]
     gain_far.wait_recv()
     gain_grad_ref[...] = flat_row(r.gain_far_out) + flat_row(r.gain_far_in)
     for i in range(3):
@@ -544,8 +562,8 @@
 
     @pl.when(half == 0)
     def _():
-        o_over.wait_send()
-        stat_over.wait_send()
+        for cp in far_back:
+            cp.wait_send()
 
 
 def hand_over_kernel(*refs):

time: 118 us -> 112 us (0.949)
  the two profiles are of different devices: /device:TPU:8 before, /device:TPU:6 now
where the time goes in v5:
time: 112 us
  Pallas kernels  111 us (99%)
    pallas_call x1, Pallas kernels, on_device(): pl.pallas_call(lambda *refs: section_kernel(tuple(scratch), *refs), out_s...  109 us
    pallas_call x1, Pallas kernels, on_device(): pl.pallas_call(hand_over_kernel, out_shape=shapes, in_specs=[hbm] * 6, ou...  2.47 us

profile of v5, /device:TPU:6, one launch (start us, length us, event | category | flops | bytes accessed | tf_op | source)
XLA Modules:
  0.0 111.9 jit_solution(4448981969851464630)
XLA Ops:
  0.6 108.7 %section.1 = (bf16[128,2048]{1,0:T(8,128)(2,1)}, bf16[128,2048]{1,0:T(8,128)(2,1)}, f32[704,128]{1,0:T(8,128)}, f32[704,128]{1,0:T(8,128)}, f32[704,128]{1,0:T(8,128)}, /*index=5*/f32[1,2048]{1,0:T(1,128)}) custom-call(bf16[128,1024]{1,0:T(8,128)(2,1)} %refs_0_.1, bf16[128,1024]{1,0:T(8,128)(2,1)} %refs_1_.1, bf16[128,1024]{1,0:T(8,128)(2,1)} %refs_2_.1, ...), custom_call_target="tpu_custom_call" | custom-call | tf_op jit(solution)/shard_map/section/pallas_call | solution.py:610
  109.3 2.5 %hand_over.1 = (bf16[128,2048]{1,0:T(8,128)(2,1)}, bf16[128,2048]{1,0:T(8,128)(2,1)}, f32[704,128]{1,0:T(8,128)}, f32[704,128]{1,0:T(8,128)}, f32[704,128]{1,0:T(8,128)}, /*index=5*/f32[1,2048]{1,0:T(1,128)}) custom-call(bf16[128,2048]{1,0:T(8,128)(2,1)} %get-tuple-element.18.refs_0_, bf16[128,2048]{1,0:T(8,128)(2,1)} %get-tuple-element.19.refs_1_, ...), custom_call_target="tpu_custom_call" | custom-call | tf_op jit(solution)/shard_map/hand_over/pallas_call | solution.py:624

commit v6 on v5

--- a/solution.py
+++ b/solution.py
@@ -67,9 +67,9 @@
         "ng": vmem((group, D), bf16),
         "gg": vmem((group, D), bf16),
         "hidden_grad": vmem((group, hid), f32),
-        "ng_all": vmem((8 * group, 2 * HEAD), bf16),
-        "gg_all": vmem((8 * group, 2 * HEAD), bf16),
-        "hgu": vmem((3, 8, group, hid), bf16),
+        "ng_all": vmem((4 * group, 4 * HEAD), bf16),
+        "gg_all": vmem((4 * group, 4 * HEAD), bf16),
+        "hgu": vmem((3, 4, group, hid), bf16),
         "down_out": vmem((TP, crows, D), bf16),
         "down_in": vmem((TP, crows, D), bf16),
         "norm_out": vmem((TP, crows, D), bf16),
@@ -82,7 +82,9 @@
         "gain_half": vmem((8,) + small, f32),
         "gain_far_out": vmem(small, f32),
         "gain_far_in": vmem(small, f32),
-        "term": vmem((3, hid, 2 * HEAD), f32),
+        "term": vmem((3, hid, 4 * HEAD), f32),
+        "sib_out": vmem((3, 2, hid, HEAD), bf16),
+        "sib_in": vmem((3, 2, hid, HEAD), bf16),
         "term_out": vmem((3, hid, HEAD), bf16),
         "term_in": vmem((3, hid, HEAD), bf16),
         "send": pltpu.SemaphoreType.DMA((COPIES,)),
@@ -276,18 +278,20 @@
     own_state = (r.m_own, r.l_own, r.acc_own)
     far_state = (r.m_far, r.l_far, r.acc_far)
 
-    def arrived(first, last):
+    def own_steps(first, last):
+        @pl.loop(first, last)
+        def _(step):
+            @pl.when(block_of(step) < block)
+            def _():
+                sweep(r.q_own, own_state, step, step + 1, block_of)
+
+    def arrived(first, last, later=False):
         @pl.when(half == 0)
         def _():
             sweep(r.q_far, far_state, first, last, block_of)
 
-        @pl.when(half == 1)
-        def _():
-            @pl.loop(max(first, 1), last)
-            def _(step):
-                @pl.when(block_of(step) < block)
-                def _():
-                    sweep(r.q_own, own_state, step, step + 1, block_of)
+        if not later:
+            own_steps(max(first, 1), last)
 
     for piece in ((0, 0), (0, 1), (1, 1)):
         st = score(r.q_own, block, piece, None)
@@ -298,18 +302,21 @@
         absorb(own_state, st, jnp.max(st, axis=0, keepdims=True), block, piece)
 
     def to_columns(rows_ref, gathered, sem):
-        copies = []
+        copies, kept = [], []
         for part in range(2):
-            dst = gathered.at[aligned(block, group), part * HEAD : (part + 1) * HEAD]
-            for off in range(1, 8):
-                peer = lax.rem(block + off, 8)
-                copies.append(remote(rows_ref.at[:, lanes(part * 8 + peer)], dst, (half * 8 + peer, t)))
-            kept = pltpu.make_async_copy(
-                rows_ref.at[:, lanes(part * 8 + block)], dst, r.local.at[sem + part]
-            )
-            kept.start()
-            kept.wait()
-        return go(copies)
+            dst = gathered.at[aligned(y, group), part * 2 * HEAD : (part + 1) * 2 * HEAD]
+
+            def columns(y_index):
+                return rows_ref.at[:, aligned(part * 4 + y_index, 2 * HEAD)]
+
+            for off in range(1, 4):
+                peer = lax.rem(y + off, 4)
+                copies.append(remote(columns(peer), dst, (half * 8 + peer * 2 + core, t)))
+            kept.append(pltpu.make_async_copy(columns(y), dst, r.local.at[sem + part]))
+        go(copies)
+        for cp in go(kept):
+            cp.wait()
+        return copies
 
     landed([k_ring[2], v_ring[2]])
 
@@ -337,9 +344,9 @@
     k_last = go([remote(k_across, k_across, (sib, t))])
     landed(v_on[:1])
     v_last = go([remote(v_across, v_across, (sib, t))])
-    arrived(4, 7)
+    arrived(4, 7, later=True)
     landed(k_last + v_last)
-    arrived(7, 8)
+    arrived(7, 8, later=True)
 
     def normalized(state, out, stat):
         m_all, l_all, acc_all = state
@@ -362,8 +369,8 @@
         r.far_in[...] = jnp.zeros(r.far_in.shape, bf16)
         r.far_stat_in[:, 0:1] = jnp.full((TP, 1, tok), very_low, f32)
         r.far_stat_in[:, 1:2] = jnp.zeros((TP, 1, tok), f32)
-        sweep(r.q_own, own_state, 0, block, lambda step: step)
-
+
+    own_steps(4, 8)
     normalized(own_state, r.o_own, r.stat_own)
     back = to_group(lambda peer: r.o_own.at[:, lanes(peer)], r.own_in.at[t])
     back += to_group(lambda peer: r.stat_own.at[:, lanes(peer)], r.own_stat_in.at[t])
@@ -426,9 +433,9 @@
     up_v = lax.dot_general(r.ng[...], r.up_w[...], contract_last, preferred_element_type=f32)
     sig = jax.nn.sigmoid(gate)
     act = gate * sig
-    above, below, across = (lax.rem(y + dy, 4) * 2 + core for dy in (1, 3, 2))
+    above, below, across = (lax.rem(y + dy, 4) for dy in (1, 3, 2))
     cut = group // 2
-    parts = (pl.ds(0, cut), pl.ds(cut, cut), pl.ds(0, group))
+    parts = (pl.ds(0, cut), pl.ds(cut, cut))
 
     def ring(i, source, piece, device):
         ref = r.hgu.at[i, source, parts[piece], :]
@@ -436,49 +443,39 @@
 
     def around(i):
         return (
-            go([ring(i, block, 0, up), ring(i, block, 1, up)]),
-            go([ring(i, block, 1, down), ring(i, block, 0, down)]),
-            go([ring(i, block, 2, sib)]),
+            go([ring(i, y, 0, up), ring(i, y, 1, up)]),
+            go([ring(i, y, 1, down), ring(i, y, 0, down)]),
         )
 
     rings = []
-    r.hgu[0, block] = (act * up_v).astype(bf16)
+    r.hgu[0, y] = (act * up_v).astype(bf16)
     rings.append(around(0))
-    r.hgu[1, block] = (
+    r.hgu[1, y] = (
         r.hidden_grad[...] * up_v * sig * (1.0 + gate * (1.0 - sig))
     ).astype(bf16)
     rings.append(around(1))
-    r.hgu[2, block] = (r.hidden_grad[...] * act).astype(bf16)
+    r.hgu[2, y] = (r.hidden_grad[...] * act).astype(bf16)
     rings.append(around(2))
 
-    part = jnp.dot(r.hgu[0, block], r.down_w[...], preferred_element_type=f32)
+    part = jnp.dot(r.hgu[0, y], r.down_w[...], preferred_element_type=f32)
     r.down_out[...] = part.astype(bf16).reshape(r.down_out.shape)
     r.down_in[t] = r.down_out[t]
     down_sum = to_group(lambda peer: r.down_out.at[peer], r.down_in.at[t])
-    part = jnp.dot(r.hgu[1, block], r.gate_w[...], preferred_element_type=f32) + jnp.dot(
-        r.hgu[2, block], r.up_w[...], preferred_element_type=f32
+    part = jnp.dot(r.hgu[1, y], r.gate_w[...], preferred_element_type=f32) + jnp.dot(
+        r.hgu[2, y], r.up_w[...], preferred_element_type=f32
     )
     r.norm_out[...] = part.astype(bf16).reshape(r.norm_out.shape)
     r.norm_in[t] = r.norm_out[t]
     norm_sum = to_group(lambda peer: r.norm_out.at[peer], r.norm_in.at[t])
 
     def pass_on(i):
-        ring_up, ring_down, _ = rings[i]
+        ring_up, ring_down = rings[i]
         landed(ring_up[:1])
         first = go([ring(i, below, 0, up)])
         landed(ring_down[:1])
-        first += go([ring(i, above, 1, down)])
-        landed(ring_up[1:])
-        rest = go([ring(i, below, 2, sib)])
-        landed(ring_down[1:])
-        rest += go([ring(i, above, 2, sib)])
-        return first, rest
-
-    def pass_last(i):
-        landed(on[i][0])
-        return go([ring(i, across, 2, sib)])
-
-    on, last = [pass_on(0)], []
+        return first + go([ring(i, above, 1, down)])
+
+    on = [pass_on(0)]
 
     landed(down_sum)
     coarse_out = coarse + jnp.sum(r.down_in[...].astype(f32), axis=0)
@@ -489,7 +486,6 @@
         .astype(bf16)
     )
     on.append(pass_on(1))
-    last.append(pass_last(0))
 
     landed(norm_sum)
     normed_grad = jnp.sum(r.norm_in[...].astype(f32), axis=0)
@@ -505,21 +501,29 @@
     gain_sum = to_group(lambda peer: r.gain_out, r.gain_in.at[t])
 
     on.append(pass_on(2))
-    last.append(pass_last(1))
 
     outs = (down_grad_ref, gate_grad_ref, up_grad_ref)
 
     def term(i):
-        landed(rings[i][2] + on[i][1] + last[i])
+        landed(rings[i][0][1:] + rings[i][1][1:] + on[i])
         right = r.gg_all if i == 0 else r.ng_all
-        left = r.hgu[i].reshape(8 * group, hid)
+        left = r.hgu[i].reshape(4 * group, hid)
         r.term[i] = lax.dot_general(left, right[...], contract_first, preferred_element_type=f32)
-        r.term_out[i] = r.term[i, :, lanes(1 - half)].astype(bf16)
-        return go([remote(r.term_out.at[i], r.term_in.at[i], (partner, t))])
+        for p in range(2):
+            r.sib_out[i, p] = r.term[i, :, lanes(2 * p + 1 - core)].astype(bf16)
+        return go([remote(r.sib_out.at[i], r.sib_in.at[i], (sib, t))])
+
+    def join(i):
+        landed(to_sib[i : i + 1])
+        r.term_out[i] = (
+            r.term[i, :, lanes(2 * (1 - half) + core)] + r.sib_in[i, 1 - half].astype(f32)
+        ).astype(bf16)
+        copies = go([remote(r.term_out.at[i], r.term_in.at[i], (partner, t))])
+        outs[i][...] = r.term[i, :, lanes(2 * half + core)] + r.sib_in[i, half].astype(f32)
+        return copies
 
     landed(grad_columns)
-    terms = term(0)
-    last.append(pass_last(2))
+    to_sib = term(0)
 
     landed(gain_sum)
     r.gain_mid[...] = jnp.sum(r.gain_in[...], axis=0)
@@ -529,7 +533,8 @@
         for off in range(1, 8)
     ])
     landed(norm_columns)
-    terms += term(1)
+    to_sib += term(1)
+    terms = join(0)
 
     follow.wait_recv()
     following = jnp.where(flat < number - 1, flat_row(r.follow_in), 0.0)
@@ -540,13 +545,13 @@
         (r.cot[...].astype(f32).reshape(spread) + contrib / SHORTEN).reshape(tok, D).astype(bf16)
     )
 
-    terms += term(2)
+    to_sib += term(2)
+    terms += join(1)
     landed(gain_group)
     r.gain_far_out[...] = jnp.sum(r.gain_half[...], axis=0)
     gain_far = remote(r.gain_far_out, r.gain_far_in, (partner, t))
     gain_far.start()
-    for i in range(3):
-        outs[i][...] = r.term[i, :, lanes(half)]
+    terms += join(2)
     gain_far.wait_recv()
     gain_grad_ref[...] = flat_row(r.gain_far_out) + flat_row(r.gain_far_in)
     for i in range(3):

time: 112 us -> 112 us (level)
  the two profiles are of different devices: /device:TPU:6 before, /device:TPU:0 now
where the time goes in v6:
time: 112 us; the launch traced here: 110 us
  Pallas kernels  110 us (98%)
    pallas_call x1, Pallas kernels, on_device(): pl.pallas_call(lambda *refs: section_kernel(tuple(scratch), *refs), out_s...  107 us
    pallas_call x1, Pallas kernels, on_device(): pl.pallas_call(hand_over_kernel, out_shape=shapes, in_specs=[hbm] * 6, ou...  2.47 us

profile of v6, /device:TPU:0, one launch (start us, length us, event | category | flops | bytes accessed | tf_op | source)
XLA Modules:
  0.0 110.4 jit_solution(15787183901050089561)
XLA Ops:
  0.6 107.2 %section.1 = (bf16[128,2048]{1,0:T(8,128)(2,1)}, bf16[128,2048]{1,0:T(8,128)(2,1)}, f32[704,128]{1,0:T(8,128)}, f32[704,128]{1,0:T(8,128)}, f32[704,128]{1,0:T(8,128)}, /*index=5*/f32[1,2048]{1,0:T(1,128)}) custom-call(bf16[128,1024]{1,0:T(8,128)(2,1)} %refs_0_.1, bf16[128,1024]{1,0:T(8,128)(2,1)} %refs_1_.1, bf16[128,1024]{1,0:T(8,128)(2,1)} %refs_2_.1, ...), custom_call_target="tpu_custom_call" | custom-call | tf_op jit(solution)/shard_map/section/pallas_call | solution.py:615
  107.8 2.5 %hand_over.1 = (bf16[128,2048]{1,0:T(8,128)(2,1)}, bf16[128,2048]{1,0:T(8,128)(2,1)}, f32[704,128]{1,0:T(8,128)}, f32[704,128]{1,0:T(8,128)}, f32[704,128]{1,0:T(8,128)}, /*index=5*/f32[1,2048]{1,0:T(1,128)}) custom-call(bf16[128,2048]{1,0:T(8,128)(2,1)} %get-tuple-element.18.refs_0_, bf16[128,2048]{1,0:T(8,128)(2,1)} %get-tuple-element.19.refs_1_, ...), custom_call_target="tpu_custom_call" | custom-call | tf_op jit(solution)/shard_map/hand_over/pallas_call | solution.py:629

commit v7 on v6

--- a/solution.py
+++ b/solution.py
@@ -13,7 +13,7 @@
 MESH = pl.DeviceIdType.MESH
 TP = 8
 WIDE = 512
-COPIES = 190
+COPIES = 200
 
 contract_last = (((1,), (1,)), ((), ()))
 contract_first = (((0,), (0,)), ((), ()))
@@ -59,9 +59,17 @@
         "far_stat_in": vmem((TP, 8, tok), f32),
         "att": vmem((TP * HEAD, tok), bf16),
         "stream": vmem((tok, D), bf16),
-        "border_out": vmem(small, f32),
-        "border_in": vmem(small, f32),
-        "coarse_b": vmem((crows, D), bf16),
+        "edge_out": vmem(small, f32),
+        "edge_in": vmem(small, f32),
+        "fine_rows": vmem((crows, D), f32),
+        "fine_pool": vmem((crows, D), bf16),
+        "fine_all": vmem((group, D), bf16),
+        "pool_out": vmem((crows, TP * HEAD), bf16),
+        "pool_all": vmem((TP, crows, TP * HEAD), bf16),
+        "rim_out": vmem((TP, HEAD), f32),
+        "rim_in": vmem((TP, TP, HEAD), f32),
+        "rim_prev": vmem((TP, HEAD), f32),
+        "coarse_all": vmem((group, D), f32),
         "coarse_grad": vmem((crows, D), f32),
         "coarse_grad_b": vmem((crows, D), bf16),
         "ng": vmem((group, D), bf16),
@@ -135,7 +143,7 @@
     peers = [(s, lax.rem(t + off, TP)) for off in range(1, TP)]
     peers += [(half * 8 + lax.rem(block + off, 8), t) for off in range(1, 8)]
     peers += [(partner, lax.rem(t + off, TP)) for off in range(TP)] + [after, before]
-    for peer in peers:
+    for peer in peers + [(lax.rem(s + 15, 16), TP - 1)]:
         pl.semaphore_signal(barrier, inc=1, device_id=peer, device_id_type=MESH)
     for ref, value in ((r.m_own, very_low), (r.l_own, 0.0), (r.acc_own, 0.0),
                        (r.m_far, very_low), (r.l_far, 0.0), (r.acc_far, 0.0)):
@@ -145,14 +153,15 @@
         r.vt_src[h] = r.v_in[:, h * HEAD : (h + 1) * HEAD].astype(f32).T.astype(bf16)
     loads["k_in"].wait()
     loads["q_in"].wait()
-    pl.semaphore_wait(barrier, len(peers))
+    pl.semaphore_wait(barrier, len(peers) + TP * (t // (TP - 1)))
 
     used, sometimes = [], []
 
-    def remote(src, dst, device, always=True):
+    def remote(src, dst, device, always=True, arrival=None):
         kind = len(used) + len(sometimes)
+        arrival = kind if arrival is None else arrival
         cp = pltpu.make_async_remote_copy(
-            src_ref=src, dst_ref=dst, send_sem=r.send.at[kind], recv_sem=r.recv.at[kind],
+            src_ref=src, dst_ref=dst, send_sem=r.send.at[kind], recv_sem=r.recv.at[arrival],
             device_id=device, device_id_type=MESH,
         )
         (used if always else sometimes).append(cp)
@@ -198,6 +207,7 @@
     ])
 
     load("cot", cot_hbm)
+    load("fine", fine_hbm)
 
     mine = aligned(t, crows)
     row = lax.broadcasted_iota(jnp.int32, (crows, tok), 0)
@@ -224,10 +234,21 @@
 
     grad_gather = to_group(lambda peer: r.coarse_grad_b, r.gg.at[mine, :])
     load("out_w", out_hbm)
-    load("fine", fine_hbm)
     load("down_w", down_hbm)
     load("gate_w", gate_hbm)
     load("up_w", up_hbm)
+
+    row = lax.broadcasted_iota(jnp.int32, (crows + 8, tok), 0)
+    col = lax.broadcasted_iota(jnp.int32, (crows + 8, tok), 1)
+    window = jnp.where((col >= row * SHORTEN - (SHORTEN - 1)) & (col <= row * SHORTEN), 1.0, 0.0)
+    window = window.astype(bf16)
+    first_row = lax.broadcasted_iota(jnp.int32, (crows, 1), 0) == 0
+    loads["fine"].wait()
+    pooled = jnp.dot(window, r.fine[...], preferred_element_type=f32)
+    r.fine_rows[...] = pooled[:crows]
+    fold_row(r.edge_out, pooled[crows : crows + 1])
+    edge_copy = remote(r.edge_out, r.edge_in, after)
+    edge_copy.start()
 
     def block_of(step):
         j = step // 2
@@ -345,6 +366,11 @@
     landed(v_on[:1])
     v_last = go([remote(v_across, v_across, (sib, t))])
     arrived(4, 7, later=True)
+    edge_copy.wait_recv()
+    edge = jnp.where(flat > 0, flat_row(r.edge_in), 0.0)
+    r.fine_pool[...] = (r.fine_rows[...] + jnp.where(first_row, edge, 0.0)).astype(bf16)
+    r.fine_all[mine, :] = r.fine_pool[...]
+    fine_gather = to_group(lambda peer: r.fine_pool, r.fine_all.at[mine, :])
     landed(k_last + v_last)
     arrived(7, 8, later=True)
 
@@ -383,7 +409,6 @@
     for cp in kept:
         cp.wait()
     loads["out_w"].wait()
-    loads["fine"].wait()
     landed(back)
 
     @pl.when(half == 1)
@@ -400,25 +425,24 @@
         r.att[h * HEAD : (h + 1) * HEAD] = (
             r.own_in[h].astype(f32) * (own_l / total) + r.far_in[h].astype(f32) * (far_l / total)
         ).astype(bf16)
-    projected = lax.dot_general(r.att[...], r.out_w[...], contract_first, preferred_element_type=f32)
-    r.stream[...] = (r.fine[...].astype(f32) + projected).astype(bf16)
-    row = lax.broadcasted_iota(jnp.int32, (crows + 8, tok), 0)
-    col = lax.broadcasted_iota(jnp.int32, (crows + 8, tok), 1)
-    window = jnp.where((col >= row * SHORTEN - (SHORTEN - 1)) & (col <= row * SHORTEN), 1.0, 0.0)
-    coarse = jnp.dot(window.astype(bf16), r.stream[...], preferred_element_type=f32)
-    fold_row(r.border_out, coarse[crows : crows + 1])
-    border_copy = remote(r.border_out, r.border_in, after)
-    border_copy.start()
-    border_copy.wait_recv()
-    edge = jnp.where(flat > 0, flat_row(r.border_in), 0.0)
-    first = lax.broadcasted_iota(jnp.int32, (crows, D), 0) == 0
-    coarse = coarse[:crows] + jnp.where(first, edge, 0.0)
-    coarse = coarse / SHORTEN
-    rstd = lax.rsqrt(jnp.mean(coarse * coarse, axis=-1, keepdims=True) + 1e-05)
-    base = coarse * rstd
-    r.coarse_b[...] = (base * gain_ref[...]).astype(bf16)
-    r.ng[mine, :] = r.coarse_b[...]
-    norm_gather = to_group(lambda peer: r.coarse_b, r.ng.at[mine, :])
+    pooled = lax.dot_general(window, r.att[...], contract_last, preferred_element_type=f32)
+    r.pool_out[...] = pooled[:crows].astype(bf16)
+    r.pool_all[t] = r.pool_out[...]
+    for i in range(TP):
+        r.rim_out[i : i + 1, :] = pooled[crows : crows + 1, i * HEAD : (i + 1) * HEAD]
+    r.rim_in[t] = r.rim_out[...]
+    pool_gather = to_group(lambda peer: r.pool_out, r.pool_all.at[t])
+    pool_gather += to_group(lambda peer: r.rim_out, r.rim_in.at[t])
+    rim_kind = len(used) + len(sometimes)
+    rim_next = [
+        remote(r.rim_out, r.rim_prev, (lax.rem(s + 1, 16), lax.rem(t + off, TP)), always=False,
+               arrival=rim_kind)
+        for off in range(TP)
+    ]
+
+    @pl.when(t == TP - 1)
+    def _():
+        go(rim_next)
 
     loads["down_w"].wait()
     r.hidden_grad[...] = lax.dot_general(
@@ -426,8 +450,24 @@
     )
     loads["gate_w"].wait()
     loads["up_w"].wait()
-
-    landed(norm_gather)
+    landed(fine_gather + pool_gather + rim_next[:1])
+    for i in range(TP):
+        source = r.rim_prev if i == 0 else r.rim_in.at[i - 1]
+        rim = jnp.concatenate([source[h : h + 1, :] for h in range(TP)], axis=1)
+        if i == 0:
+            rim = jnp.where(s > 0, rim, 0.0)
+        r.pool_all[i] = (r.pool_all[i].astype(f32) + jnp.where(first_row, rim, 0.0)).astype(bf16)
+    coarse_all = jnp.dot(
+        r.pool_all[...].reshape(group, TP * HEAD), r.out_w[...], preferred_element_type=f32
+    )
+    coarse_all = (coarse_all + r.fine_all[...].astype(f32)) / SHORTEN
+    r.coarse_all[...] = coarse_all
+    rstd_all = lax.rsqrt(jnp.mean(coarse_all * coarse_all, axis=-1, keepdims=True) + 1e-05)
+    r.ng[...] = (coarse_all * rstd_all * gain_ref[...]).astype(bf16)
+    coarse = r.coarse_all[mine, :]
+    rstd = lax.rsqrt(jnp.mean(coarse * coarse, axis=-1, keepdims=True) + 1e-05)
+    base = coarse * rstd
+
     norm_columns = to_columns(r.ng, r.ng_all, 15)
     gate = lax.dot_general(r.ng[...], r.gate_w[...], contract_last, preferred_element_type=f32)
     up_v = lax.dot_general(r.ng[...], r.up_w[...], contract_last, preferred_element_type=f32)
@@ -467,6 +507,12 @@
     r.norm_out[...] = part.astype(bf16).reshape(r.norm_out.shape)
     r.norm_in[t] = r.norm_out[t]
     norm_sum = to_group(lambda peer: r.norm_out.at[peer], r.norm_in.at[t])
+    fold_row(r.gain_out, jnp.sum(part * (r.coarse_all[...] * rstd_all), axis=0, keepdims=True))
+    r.gain_in[t] = r.gain_out[...]
+    gain_sum = to_group(lambda peer: r.gain_out, r.gain_in.at[t])
+
+    projected = lax.dot_general(r.att[...], r.out_w[...], contract_first, preferred_element_type=f32)
+    r.stream[...] = (r.fine[...].astype(f32) + projected).astype(bf16)
 
     def pass_on(i):
         ring_up, ring_down = rings[i]
@@ -476,6 +522,14 @@
         return first + go([ring(i, above, 1, down)])
 
     on = [pass_on(0)]
+
+    landed(gain_sum)
+    r.gain_mid[...] = jnp.sum(r.gain_in[...], axis=0)
+    r.gain_half[block] = r.gain_mid[...]
+    gain_group = go([
+        remote(r.gain_mid, r.gain_half.at[block], (half * 8 + lax.rem(block + off, 8), t))
+        for off in range(1, 8)
+    ])
 
     landed(down_sum)
     coarse_out = coarse + jnp.sum(r.down_in[...].astype(f32), axis=0)
@@ -496,9 +550,6 @@
     fold_row(r.follow_out, coarse_total[0:1])
     follow = remote(r.follow_out, r.follow_in, before)
     follow.start()
-    fold_row(r.gain_out, jnp.sum(normed_grad * base, axis=0, keepdims=True))
-    r.gain_in[t] = r.gain_out[...]
-    gain_sum = to_group(lambda peer: r.gain_out, r.gain_in.at[t])
 
     on.append(pass_on(2))
 
@@ -525,13 +576,6 @@
     landed(grad_columns)
     to_sib = term(0)
 
-    landed(gain_sum)
-    r.gain_mid[...] = jnp.sum(r.gain_in[...], axis=0)
-    r.gain_half[block] = r.gain_mid[...]
-    gain_group = go([
-        remote(r.gain_mid, r.gain_half.at[block], (half * 8 + lax.rem(block + off, 8), t))
-        for off in range(1, 8)
-    ])
     landed(norm_columns)
     to_sib += term(1)
     terms = join(0)
@@ -560,6 +604,11 @@
 
     for cp in used:
         cp.wait_send()
+
+    @pl.when(t == TP - 1)
+    def _():
+        for cp in rim_next:
+            cp.wait_send()
 
     @pl.when(half == 1)
     def _():

time: 112 us -> 111 us (level)
  Pallas kernels: 110 us -> 108 us
    pallas_call x1, Pallas kernels: 107 us -> 106 us  [on_device(): pl.pallas_call(lambda *refs: section_kernel(tuple(scratch), *refs), out_s...]
where the time goes in v7:
time: 111 us; the launch traced here: 109 us
  Pallas kernels  108 us (97%)
    pallas_call x1, Pallas kernels, on_device(): pl.pallas_call(lambda *refs: section_kernel(tuple(scratch), *refs), out_s...  106 us
    pallas_call x1, Pallas kernels, on_device(): pl.pallas_call(hand_over_kernel, out_shape=shapes, in_specs=[hbm] * 6, ou...  2.47 us

profile of v7, /device:TPU:0, one launch (start us, length us, event | category | flops | bytes accessed | tf_op | source)
XLA Modules:
  0.0 109.1 jit_solution(8670207236173310713)
XLA Ops:
  0.6 105.9 %section.1 = (bf16[128,2048]{1,0:T(8,128)(2,1)}, bf16[128,2048]{1,0:T(8,128)(2,1)}, f32[704,128]{1,0:T(8,128)}, f32[704,128]{1,0:T(8,128)}, f32[704,128]{1,0:T(8,128)}, /*index=5*/f32[1,2048]{1,0:T(1,128)}) custom-call(bf16[128,1024]{1,0:T(8,128)(2,1)} %refs_0_.1, bf16[128,1024]{1,0:T(8,128)(2,1)} %refs_1_.1, bf16[128,1024]{1,0:T(8,128)(2,1)} %refs_2_.1, ...), custom_call_target="tpu_custom_call" | custom-call | tf_op jit(solution)/shard_map/section/pallas_call | solution.py:664
  106.5 2.5 %hand_over.1 = (bf16[128,2048]{1,0:T(8,128)(2,1)}, bf16[128,2048]{1,0:T(8,128)(2,1)}, f32[704,128]{1,0:T(8,128)}, f32[704,128]{1,0:T(8,128)}, f32[704,128]{1,0:T(8,128)}, /*index=5*/f32[1,2048]{1,0:T(1,128)}) custom-call(bf16[128,2048]{1,0:T(8,128)(2,1)} %get-tuple-element.18.refs_0_, bf16[128,2048]{1,0:T(8,128)(2,1)} %get-tuple-element.19.refs_1_, ...), custom_call_target="tpu_custom_call" | custom-call | tf_op jit(solution)/shard_map/hand_over/pallas_call | solution.py:678

commit v8 on v7

--- a/solution.py
+++ b/solution.py
@@ -13,7 +13,7 @@
 MESH = pl.DeviceIdType.MESH
 TP = 8
 WIDE = 512
-COPIES = 200
+COPIES = 210
 
 contract_last = (((1,), (1,)), ((), ()))
 contract_first = (((0,), (0,)), ((), ()))
@@ -39,6 +39,7 @@
         "vt_src": vmem((TP, HEAD, tok), bf16),
         "q_own": vmem((rows, HEAD), bf16),
         "q_far": vmem((rows, HEAD), bf16),
+        "q_work": vmem((rows, HEAD), bf16),
         "k_all": vmem((8, rows, HEAD), bf16),
         "vt_all": vmem((8, HEAD, rows), bf16),
         "scores": vmem((2, WIDE, WIDE), f32),
@@ -120,6 +121,8 @@
     up = half * 8 + lax.rem(y + 1, 4) * 2 + core
     down = half * 8 + lax.rem(y + 3, 4) * 2 + core
     partner = (1 - half) * 8 + block
+    mirror_block = (3 - y) * 2 + core
+    mirror = half * 8 + mirror_block
     number = lax.axis_size("seq") * TP
     flat = s * TP + t
     after, before = lax.rem(flat + 1, number), lax.rem(flat + number - 1, number)
@@ -145,6 +148,12 @@
     peers += [(partner, lax.rem(t + off, TP)) for off in range(TP)] + [after, before]
     for peer in peers + [(lax.rem(s + 15, 16), TP - 1)]:
         pl.semaphore_signal(barrier, inc=1, device_id=peer, device_id_type=MESH)
+
+    @pl.when(t >= TP // 2)
+    def _():
+        for h in range(TP):
+            pl.semaphore_signal(barrier, inc=1, device_id=(mirror, h), device_id_type=MESH)
+
     for ref, value in ((r.m_own, very_low), (r.l_own, 0.0), (r.acc_own, 0.0),
                        (r.m_far, very_low), (r.l_far, 0.0), (r.acc_far, 0.0)):
         ref[...] = jnp.full(ref.shape, value, f32)
@@ -153,7 +162,7 @@
         r.vt_src[h] = r.v_in[:, h * HEAD : (h + 1) * HEAD].astype(f32).T.astype(bf16)
     loads["k_in"].wait()
     loads["q_in"].wait()
-    pl.semaphore_wait(barrier, len(peers) + TP * (t // (TP - 1)))
+    pl.semaphore_wait(barrier, len(peers) + TP // 2 + TP * (t // (TP - 1)))
 
     used, sometimes = [], []
 
@@ -226,6 +235,10 @@
     landed(v_copies)
     v_ring = go([remote(v_mine, v_mine, (device, t)) for device in (down, up, sib)])
     landed(q_copies)
+    low, high = pl.ds(0, WIDE), pl.ds(WIDE, WIDE)
+    q_swap = remote(r.q_own.at[high, :], r.q_work.at[high, :], (mirror, t))
+    q_swap.start()
+    r.q_work[low, :] = r.q_own[low, :]
     q_over = remote(r.q_own, r.q_far, (partner, t), always=False)
 
     @pl.when(half == 1)
@@ -281,9 +294,8 @@
             preferred_element_type=f32,
         )
 
-    pieces = [(kk, u) for kk in range(2) for u in range(2)]
-
-    def sweep(q_all, state, first, last, index):
+    def sweep(q_all, state, first, last, index, columns=(0, 1)):
+        pieces = [(kk, u) for kk in range(2) for u in columns]
         score(q_all, index(first), pieces[0], 0)
 
         @pl.loop(first, last)
@@ -299,28 +311,20 @@
     own_state = (r.m_own, r.l_own, r.acc_own)
     far_state = (r.m_far, r.l_far, r.acc_far)
 
-    def own_steps(first, last):
-        @pl.loop(first, last)
-        def _(step):
-            @pl.when(block_of(step) < block)
-            def _():
-                sweep(r.q_own, own_state, step, step + 1, block_of)
-
-    def arrived(first, last, later=False):
+    def arrived(first, last):
         @pl.when(half == 0)
         def _():
             sweep(r.q_far, far_state, first, last, block_of)
 
-        if not later:
-            own_steps(max(first, 1), last)
-
-    for piece in ((0, 0), (0, 1), (1, 1)):
-        st = score(r.q_own, block, piece, None)
-        if piece[0] == piece[1]:
+    def fold_own(key_block, piece, diagonal):
+        st = score(r.q_work, key_block, piece, None)
+        if diagonal:
             key_pos = lax.broadcasted_iota(jnp.int32, st.shape, 0)
             query_pos = lax.broadcasted_iota(jnp.int32, st.shape, 1)
             st = jnp.where(key_pos <= query_pos, st, very_low)
-        absorb(own_state, st, jnp.max(st, axis=0, keepdims=True), block, piece)
+        absorb(own_state, st, jnp.max(st, axis=0, keepdims=True), key_block, piece)
+
+    fold_own(block, (0, 0), True)
 
     def to_columns(rows_ref, gathered, sem):
         copies, kept = [], []
@@ -365,14 +369,14 @@
     k_last = go([remote(k_across, k_across, (sib, t))])
     landed(v_on[:1])
     v_last = go([remote(v_across, v_across, (sib, t))])
-    arrived(4, 7, later=True)
+    arrived(4, 7)
     edge_copy.wait_recv()
     edge = jnp.where(flat > 0, flat_row(r.edge_in), 0.0)
     r.fine_pool[...] = (r.fine_rows[...] + jnp.where(first_row, edge, 0.0)).astype(bf16)
     r.fine_all[mine, :] = r.fine_pool[...]
     fine_gather = to_group(lambda peer: r.fine_pool, r.fine_all.at[mine, :])
     landed(k_last + v_last)
-    arrived(7, 8, later=True)
+    arrived(7, 8)
 
     def normalized(state, out, stat):
         m_all, l_all, acc_all = state
@@ -396,20 +400,50 @@
         r.far_stat_in[:, 0:1] = jnp.full((TP, 1, tok), very_low, f32)
         r.far_stat_in[:, 1:2] = jnp.zeros((TP, 1, tok), f32)
 
-    own_steps(4, 8)
+    q_swap.wait_recv()
+    sweep(r.q_work, own_state, 0, block, lambda step: step, (0,))
+    sweep(r.q_work, own_state, 0, mirror_block, lambda step: step, (1,))
+    fold_own(mirror_block, (0, 1), False)
+    fold_own(mirror_block, (1, 1), True)
     normalized(own_state, r.o_own, r.stat_own)
-    back = to_group(lambda peer: r.o_own.at[:, lanes(peer)], r.own_in.at[t])
-    back += to_group(lambda peer: r.stat_own.at[:, lanes(peer)], r.own_stat_in.at[t])
-    kept = go([
-        pltpu.make_async_copy(r.o_own.at[:, lanes(t)], r.own_in.at[t], r.local.at[14]),
-        pltpu.make_async_copy(r.stat_own.at[:, lanes(t)], r.own_stat_in.at[t], r.local.at[17]),
-    ])
+
+    def row_owner(peer):
+        return (s + (peer // (TP // 2)) * (mirror - s), peer)
+
+    back = []
+    for off in range(1, TP):
+        peer = lax.rem(t + off, TP)
+        back += [
+            remote(r.o_own.at[:, lanes(peer)], r.own_in.at[t], row_owner(peer)),
+            remote(r.stat_own.at[:, lanes(peer)], r.own_stat_in.at[t], row_owner(peer)),
+        ]
+    go(back)
+    swapped = [
+        remote(r.o_own.at[:, lanes(t)], r.own_in.at[t], (mirror, t), always=False),
+        remote(r.stat_own.at[:, lanes(t)], r.own_stat_in.at[t], (mirror, t), always=False),
+    ]
+
+    @pl.when(t < TP // 2)
+    def _():
+        kept = go([
+            pltpu.make_async_copy(r.o_own.at[:, lanes(t)], r.own_in.at[t], r.local.at[14]),
+            pltpu.make_async_copy(r.stat_own.at[:, lanes(t)], r.own_stat_in.at[t], r.local.at[17]),
+        ])
+        for cp in kept:
+            cp.wait()
+
+    @pl.when(t >= TP // 2)
+    def _():
+        go(swapped)
+
     landed(grad_gather)
     grad_columns = to_columns(r.gg, r.gg_all, 12)
-    for cp in kept:
-        cp.wait()
     loads["out_w"].wait()
     landed(back)
+
+    @pl.when(t >= TP // 2)
+    def _():
+        landed(swapped)
 
     @pl.when(half == 1)
     def _():
@@ -608,6 +642,11 @@
     @pl.when(t == TP - 1)
     def _():
         for cp in rim_next:
+            cp.wait_send()
+
+    @pl.when(t >= TP // 2)
+    def _():
+        for cp in swapped:
             cp.wait_send()
 
     @pl.when(half == 1)

time: 111 us -> 113 us (1.018)
  Pallas kernels: 108 us -> 111 us
    pallas_call x1, Pallas kernels: 106 us -> 109 us  [on_device(): pl.pallas_call(lambda *refs: section_kernel(tuple(scratch), *refs), out_s...]
where the time goes in v8:
time: 113 us; the launch traced here: 112 us
  Pallas kernels  111 us (98%)
    pallas_call x1, Pallas kernels, on_device(): pl.pallas_call(lambda *refs: section_kernel(tuple(scratch), *refs), out_s...  109 us
    pallas_call x1, Pallas kernels, on_device(): pl.pallas_call(hand_over_kernel, out_shape=shapes, in_specs=[hbm] * 6, ou...  2.47 us

profile of v8, /device:TPU:0, one launch (start us, length us, event | category | flops | bytes accessed | tf_op | source)
XLA Modules:
  0.0 111.8 jit_solution(15632878435557931004)
XLA Ops:
  0.6 108.5 %section.1 = (bf16[128,2048]{1,0:T(8,128)(2,1)}, bf16[128,2048]{1,0:T(8,128)(2,1)}, f32[704,128]{1,0:T(8,128)}, f32[704,128]{1,0:T(8,128)}, f32[704,128]{1,0:T(8,128)}, /*index=5*/f32[1,2048]{1,0:T(1,128)}) custom-call(bf16[128,1024]{1,0:T(8,128)(2,1)} %refs_0_.1, bf16[128,1024]{1,0:T(8,128)(2,1)} %refs_1_.1, bf16[128,1024]{1,0:T(8,128)(2,1)} %refs_2_.1, ...), custom_call_target="tpu_custom_call" | custom-call | tf_op jit(solution)/shard_map/section/pallas_call | solution.py:703
  109.2 2.5 %hand_over.1 = (bf16[128,2048]{1,0:T(8,128)(2,1)}, bf16[128,2048]{1,0:T(8,128)(2,1)}, f32[704,128]{1,0:T(8,128)}, f32[704,128]{1,0:T(8,128)}, f32[704,128]{1,0:T(8,128)}, /*index=5*/f32[1,2048]{1,0:T(1,128)}) custom-call(bf16[128,2048]{1,0:T(8,128)(2,1)} %get-tuple-element.18.refs_0_, bf16[128,2048]{1,0:T(8,128)(2,1)} %get-tuple-element.19.refs_1_, ...), custom_call_target="tpu_custom_call" | custom-call | tf_op jit(solution)/shard_map/hand_over/pallas_call | solution.py:717

commit v9 on v7

--- a/solution.py
+++ b/solution.py
@@ -580,6 +580,9 @@
     to_sib += term(1)
     terms = join(0)
 
+    to_sib += term(2)
+    terms += join(1)
+
     follow.wait_recv()
     following = jnp.where(flat < number - 1, flat_row(r.follow_in), 0.0)
     ahead = jnp.concatenate([coarse_total[1:], following], axis=0)
@@ -589,8 +592,6 @@
         (r.cot[...].astype(f32).reshape(spread) + contrib / SHORTEN).reshape(tok, D).astype(bf16)
     )
 
-    to_sib += term(2)
-    terms += join(1)
     landed(gain_group)
     r.gain_far_out[...] = jnp.sum(r.gain_half[...], axis=0)
     gain_far = remote(r.gain_far_out, r.gain_far_in, (partner, t))

time: 111 us -> 111 us (level)
  no operation moved by 1% of the time
where the time goes in v9:
time: 111 us; the launch traced here: 109 us
  Pallas kernels  108 us (97%)
    pallas_call x1, Pallas kernels, on_device(): pl.pallas_call(lambda *refs: section_kernel(tuple(scratch), *refs), out_s...  106 us
    pallas_call x1, Pallas kernels, on_device(): pl.pallas_call(hand_over_kernel, out_shape=shapes, in_specs=[hbm] * 6, ou...  2.47 us

profile of v9, /device:TPU:0, one launch (start us, length us, event | category | flops | bytes accessed | tf_op | source)
XLA Modules:
  0.0 109.1 jit_solution(12657621971466210732)
XLA Ops:
  0.6 105.9 %section.1 = (bf16[128,2048]{1,0:T(8,128)(2,1)}, bf16[128,2048]{1,0:T(8,128)(2,1)}, f32[704,128]{1,0:T(8,128)}, f32[704,128]{1,0:T(8,128)}, f32[704,128]{1,0:T(8,128)}, /*index=5*/f32[1,2048]{1,0:T(1,128)}) custom-call(bf16[128,1024]{1,0:T(8,128)(2,1)} %refs_0_.1, bf16[128,1024]{1,0:T(8,128)(2,1)} %refs_1_.1, bf16[128,1024]{1,0:T(8,128)(2,1)} %refs_2_.1, ...), custom_call_target="tpu_custom_call" | custom-call | tf_op jit(solution)/shard_map/section/pallas_call | solution.py:665
  106.5 2.5 %hand_over.1 = (bf16[128,2048]{1,0:T(8,128)(2,1)}, bf16[128,2048]{1,0:T(8,128)(2,1)}, f32[704,128]{1,0:T(8,128)}, f32[704,128]{1,0:T(8,128)}, f32[704,128]{1,0:T(8,128)}, /*index=5*/f32[1,2048]{1,0:T(1,128)}) custom-call(bf16[128,2048]{1,0:T(8,128)(2,1)} %get-tuple-element.18.refs_0_, bf16[128,2048]{1,0:T(8,128)(2,1)} %get-tuple-element.19.refs_1_, ...), custom_call_target="tpu_custom_call" | custom-call | tf_op jit(solution)/shard_map/hand_over/pallas_call | solution.py:679
